TPU v7x, 256 devices: a whole 4x4x8 slice. The times are simulated.
256 devices in a mesh: scene: 8 (over x, core), seq: 32 (over y, z).
Axes of the slice: x: 4, y: 4, z: 8, core: 2. Of those that a mesh axis runs over, the one named last changes fastest.
Arguments:
- tokens: bfloat16 [4096, 64, 512], P(('scene', 'seq')), parts along dimension 0, may hold values from -6 to 6
- block_counts: int32 [256], P('scene'), parts along dimension 0, may hold values from 1 to 16, 320 in all
- gains: float32 [3, 512], replicated, may hold values from 0.1 to 1.9
- qkv_time: bfloat16 [512, 1536], replicated, may hold values from -0.25 to 0.25
- out_time: bfloat16 [512, 512], replicated, may hold values from -0.25 to 0.25
- qkv_scene: bfloat16 [512, 1536], replicated, may hold values from -0.25 to 0.25
- out_scene: bfloat16 [512, 512], replicated, may hold values from -0.25 to 0.25
- mlp_in: bfloat16 [512, 2048], replicated, may hold values from -0.25 to 0.25
- mlp_out: bfloat16 [2048, 512], replicated, may hold values from -0.125 to 0.125
Outputs:
- encoded: bfloat16 [4096, 64, 512], P(('scene', 'seq')), parts along dimension 0
There are 8 independent parts, one for each index of `scene`. A program takes and returns all parts, laid end to end along the dimension named above; an argument that names none is the same for every part. Nothing has to cross between parts.
Inputs may be any that keep to these rules, and one draw needn't show every extreme that they name: Within each scene, the live agents of each aligned block of 16 slots are its first block_counts slots, the scene's counts sum to 320, and some block of the scene is full.
All inputs are finite; a program needn't handle non-finite values.
Results may differ from a plain program's by a relative error of at most 0.02.
Values may be sent and summed in bfloat16 or wider, within the bound.
No kernel may reach another device: no remote copies, remote signals or barrier semaphores. Data moves between devices by JAX's collectives and lax.ppermute only.
A program may use at most 128 MiB of HBM per device.

v0:
```python
import jax
import jax.numpy as jnp
from jax import lax
from jax.sharding import PartitionSpec as P

HEADS = 8


def rms_norm(values, gain):
    floats = values.astype(jnp.float32)
    inverse = lax.rsqrt(jnp.mean(floats * floats, axis=-1, keepdims=True) + 1e-06)
    return (floats * inverse * gain).astype(jnp.bfloat16)


def per_device(
    tokens, block_counts, gains, qkv_time, out_time, qkv_scene, out_scene, mlp_in, mlp_out
):
    agents, step_count, model_width = tokens.shape
    groups = lax.axis_size("seq")
    head_size = model_width // HEADS
    inv_root = 1.0 / float(head_size) ** 0.5
    all_agents = agents * groups
    local_steps = step_count // groups
    rows = agents * step_count
    own_count = lax.dynamic_index_in_dim(block_counts, lax.axis_index("seq"), keepdims=False)
    local_live = jnp.arange(agents, dtype=jnp.int32) < own_count
    all_slots = jnp.arange(all_agents, dtype=jnp.int32)
    all_live = all_slots % agents < jnp.repeat(block_counts, agents)
    first = rms_norm(tokens, gains[0])
    packed = jnp.dot(first.reshape(rows, model_width), qkv_time, preferred_element_type=jnp.float32)
    packed = packed.astype(jnp.bfloat16).reshape(agents, step_count, 3, HEADS, head_size)
    scores = (
        jnp.einsum(
            "ashd,athd->ahst", packed[:, :, 0], packed[:, :, 1], preferred_element_type=jnp.float32
        )
        * inv_root
    )
    weights = jax.nn.softmax(scores, axis=-1).astype(jnp.bfloat16)
    context = jnp.einsum(
        "ahst,athd->ashd", weights, packed[:, :, 2], preferred_element_type=jnp.float32
    ).astype(jnp.bfloat16)
    update = jnp.dot(
        context.reshape(rows, model_width), out_time, preferred_element_type=jnp.float32
    )
    after_time = (
        tokens.astype(jnp.float32) + update.reshape(agents, step_count, model_width)
    ).astype(jnp.bfloat16)
    second = rms_norm(after_time, gains[1])
    triples_local = jnp.dot(
        second.reshape(rows, model_width), qkv_scene, preferred_element_type=jnp.float32
    )
    triples_local = triples_local.astype(jnp.bfloat16).reshape(
        agents, groups, local_steps, 3 * model_width
    )
    triples = lax.all_to_all(triples_local, "seq", split_axis=1, concat_axis=0, tiled=True)
    count = triples.shape[2]
    split = triples.reshape(all_agents, count, 3, HEADS, head_size)
    logits = (
        jnp.einsum(
            "athd,bthd->thab", split[:, :, 0], split[:, :, 1], preferred_element_type=jnp.float32
        )
        * inv_root
    )
    logits = jnp.where(all_live[None, None, None, :], logits, -1e30)
    probs = jax.nn.softmax(logits, axis=-1).astype(jnp.bfloat16)
    mixed_ctx = jnp.einsum(
        "thab,bthd->athd", probs, split[:, :, 2], preferred_element_type=jnp.float32
    ).astype(jnp.bfloat16)
    projected = jnp.dot(
        mixed_ctx.reshape(all_agents * count, model_width),
        out_scene,
        preferred_element_type=jnp.float32,
    )
    scene_out = projected.astype(jnp.bfloat16).reshape(all_agents, 1, count, model_width)
    returned = lax.all_to_all(scene_out, "seq", split_axis=0, concat_axis=1, tiled=True).reshape(
        agents, step_count, model_width
    )
    after_scene = (after_time.astype(jnp.float32) + returned.astype(jnp.float32)).astype(
        jnp.bfloat16
    )
    third = rms_norm(after_scene, gains[2])
    hidden = jnp.maximum(
        jnp.dot(third.reshape(rows, model_width), mlp_in, preferred_element_type=jnp.float32), 0.0
    ).astype(jnp.bfloat16)
    result = after_scene.astype(jnp.float32) + jnp.dot(
        hidden, mlp_out, preferred_element_type=jnp.float32
    ).reshape(agents, step_count, model_width)
    return jnp.where(local_live[:, None, None], result, 0.0).astype(jnp.bfloat16)


def solution(mesh):
    placed = (P(("scene", "seq"), None, None), P("scene"), P(), P(), P(), P(), P(), P(), P())
    return jax.shard_map(
        per_device,
        mesh=mesh,
        in_specs=placed,
        out_specs=P(("scene", "seq"), None, None),
        check_vma=False,
    )
```

profile of v0, /device:TPU:1, one launch (start us, length us, event | category | flops | bytes accessed | tf_op | source)
XLA Modules:
  0.0 254.5 jit_solution(17728494884252839595)
XLA Ops:
  0.0 0.9 fusion.60
  0.9 1.6 fusion.10
  2.5 1.5 fusion.12
  4.0 3.5 %convolution_convert_fusion.1 = bf16[1024,1536]{1,0:T(8,128)(2,1)} fusion(bf16[1024,512]{1,0:T(8,128)(2,1)S(1)} %bitcast.86, bf16[512,1536]{1,0:T(8,128)(2,1)S(1)} %copy-done.6), kind=kOutput, calls=%fused_computation.14 | convolution fusion | flops 1612185600 | bytes 5767168 | tf_op jit(solution)/shard_map/dot_general | solution.py:30
  7.5 8.9 %reshape.91 = bf16[16,64,3,8,64]{4,3,2,1,0:T(8,128)(2,1)} reshape(bf16[1024,1536]{1,0:T(8,128)(2,1)} %convolution_convert_fusion.1) | data formatting | bytes 6291456 | tf_op jit(solution)/shard_map/reshape | solution.py:31
  16.4 5.7 %fusion.59 = (bf16[16,64,1,8,64]{4,3,2,1,0:T(8,128)(2,1)}, bf16[16,64,1,8,64]{4,3,2,1,0:T(8,128)(2,1)}, bf16[16,64,1,8,64]{4,3,2,1,0:T(8,128)(2,1)}) fusion(bf16[16,64,3,8,64]{4,3,2,1,0:T(8,128)(2,1)} %reshape.91), kind=kLoop, calls=%fused_computation.75 | loop fusion | bytes 6291456 | tf_op jit(solution)/shard_map/slice | solution.py:40
  22.1 4.1 %copy.47 = bf16[16,64,1,8,64]{1,4,3,0,2:T(8,128)(2,1)} copy(bf16[16,64,1,8,64]{4,3,2,1,0:T(8,128)(2,1)} %get-tuple-element.10) | data formatting | bytes 2097152
  26.2 3.4 %fusion.24 = f32[16,8,64,64]{2,3,1,0:T(8,128)S(1)} fusion(bf16[16,64,1,8,64]{4,3,2,1,0:T(8,128)(2,1)} %get-tuple-element.11, bf16[16,64,1,8,64]{4,3,2,1,0:T(8,128)(2,1)} %get-tuple-element.12), kind=kOutput, calls=%fused_computation.41 | convolution fusion | flops 67108864 | bytes 4194304 | tf_op jit(solution)/shard_map/ashd,athd->ahst/dot_general | solution.py:33
  29.7 6.2 %fusion.61 = (f32[16,8,64]{2,1,0:T(8,128)S(1)}, f32[16,8,64,64]{2,3,1,0:T(8,128)S(1)}) fusion(f32[16,8,64,64]{2,3,1,0:T(8,128)S(1)} %fusion.24), kind=kOutput, calls=%fused_computation.77 | output fusion | flops 2097215 | bytes 4227072 | tf_op jit(solution)/shard_map/sub | solution.py:38
  35.9 0.0 copy-start.1
  35.9 0.7 fusion.28
  36.6 0.5 copy-done.1
  37.1 0.1 copy-done.4
  37.2 0.9 fusion.14
  38.1 1.0 copy-done.2
  39.1 0.3 fusion.16
  39.4 0.5 copy-done.7
  39.9 3.5 %convolution_convert_fusion = bf16[1024,1536]{1,0:T(8,128)(2,1)} fusion(bf16[1024,512]{1,0:T(8,128)(2,1)S(1)} %bitcast.87, bf16[512,1536]{1,0:T(8,128)(2,1)S(1)} %copy-done.7), kind=kOutput, calls=%fused_computation.13 | convolution fusion | flops 1612185600 | bytes 5767168 | tf_op jit(solution)/shard_map/dot_general | solution.py:49
  43.4 7.2 %reshape.93 = bf16[16,32,2,1536]{3,2,1,0:T(2,128)(2,1)} reshape(bf16[1024,1536]{1,0:T(8,128)(2,1)} %convolution_convert_fusion) | data formatting | bytes 6291456 | tf_op jit(solution)/shard_map/reshape | solution.py:52
  50.6 6.2 %copy.34 = bf16[16,32,2,1536]{3,0,2,1:T(8,128)(2,1)} copy(bf16[16,32,2,1536]{3,2,1,0:T(2,128)(2,1)} %reshape.93) | data formatting | bytes 6291456 | tf_op jit(solution)/shard_map/reshape | solution.py:52
  56.8 12.5 %all-to-all-start = ((bf16[16,32,2,1536]{3,0,2,1:T(8,128)(2,1)}), bf16[16,32,2,1536]{3,0,2,1:T(8,128)(2,1)}, u32[]{:S(2)}, u32[]{:S(2)}) async-start(bf16[16,32,2,1536]{3,0,2,1:T(8,128)(2,1)} %copy.34), calls=%async_computation | async-start | bytes 6291456 | tf_op jit(solution)/shard_map/all_to_all | solution.py:55
  69.3 0.1 broadcast_in_dim.37
  69.3 0.1 reshape.95
  69.4 71.3 %all-to-all-done = bf16[16,32,2,1536]{3,0,2,1:T(8,128)(2,1)} async-done(((bf16[16,32,2,1536]{3,0,2,1:T(8,128)(2,1)}), bf16[16,32,2,1536]{3,0,2,1:T(8,128)(2,1)}, u32[]{:S(2)}, u32[]{:S(2)}) %all-to-all-start) | async-done | bytes 3145760 | tf_op jit(solution)/shard_map/all_to_all | solution.py:55
  140.8 3.8 %copy.35 = bf16[32,16,1,2,1536]{4,1,0,3,2:T(8,128)(2,1)} copy(bf16[32,16,1,2,1536]{4,1,3,0,2:T(8,128)(2,1)} %bitcast.12) | data formatting | bytes 6291456 | tf_op jit(solution)/shard_map/all_to_all | solution.py:55
  144.6 8.9 %reshape.94 = bf16[512,2,3,8,64]{4,3,2,0,1:T(8,128)(2,1)} reshape(bf16[32,16,1,2,1536]{4,1,0,3,2:T(8,128)(2,1)} %copy.35) | data formatting | bytes 6291456 | tf_op jit(solution)/shard_map/reshape | solution.py:57
  153.4 5.7 %fusion.58 = (bf16[512,2,1,8,64]{4,3,2,0,1:T(8,128)(2,1)}, bf16[512,2,1,8,64]{4,3,2,0,1:T(8,128)(2,1)}, bf16[512,2,1,8,64]{4,3,2,0,1:T(8,128)(2,1)}) fusion(bf16[512,2,3,8,64]{4,3,2,0,1:T(8,128)(2,1)} %reshape.94), kind=kLoop, calls=%fused_computation.74 | loop fusion | bytes 6291456 | tf_op jit(solution)/shard_map/slice | solution.py:67
  159.1 2.5 copy.50
  161.6 3.3 %copy.51 = bf16[512,2,1,8,64]{0,4,3,1,2:T(8,128)(2,1)} copy(bf16[512,2,1,8,64]{4,3,2,0,1:T(8,128)(2,1)} %get-tuple-element.8) | data formatting | bytes 2097152
  165.0 3.3 %copy.52 = bf16[512,2,1,8,64]{0,4,3,1,2:T(8,128)(2,1)} copy(bf16[512,2,1,8,64]{4,3,2,0,1:T(8,128)(2,1)} %get-tuple-element.9) | data formatting | bytes 2097152
  168.3 11.0 %fusion.62 = (f32[2,8,512]{2,1,0:T(8,128)S(1)}, f32[2,8,512,512]{2,3,1,0:T(8,128)}) fusion(pred[512]{0:T(512)(128)(4,1)S(1)} %fusion.49, bf16[512,2,1,8,64]{0,4,3,1,2:T(8,128)(2,1)} %copy.52, bf16[512,2,1,8,64]{0,4,3,1,2:T(8,128)(2,1)} %copy.51), kind=kOutput, calls=%fused_computation.78 | convolution fusion | flops 553648640 | bytes 18907648 | tf_op jit(solution)/shard_map/sub | solution.py:65
  179.3 8.3 %fusion.34 = bf16[512,2,8,64]{0,3,2,1:T(8,128)(2,1)} fusion(f32[2,8,512,512]{2,3,1,0:T(8,128)} %get-tuple-element.21, f32[2,8,512]{2,1,0:T(8,128)S(1)} %get-tuple-element.20, bf16[512,2,1,8,64]{0,4,3,1,2:T(8,128)(2,1)S(1)} %copy.50), kind=kOutput, calls=%fused_computation.51 | convolution fusion | flops 545783808 | bytes 18907136 | tf_op jit(solution)/shard_map/thab,bthd->athd/dot_general | solution.py:66
  187.6 3.9 %copy.40 = bf16[512,2,8,64]{3,2,1,0:T(8,128)(2,1)} copy(bf16[512,2,8,64]{0,3,2,1:T(8,128)(2,1)} %fusion.34) | data formatting | bytes 2097152 | tf_op jit(solution)/shard_map/convert_element_type | solution.py:68
  191.5 3.2 %reshape.96 = bf16[1024,512]{1,0:T(8,128)(2,1)S(1)} reshape(bf16[512,2,8,64]{3,2,1,0:T(8,128)(2,1)} %copy.40) | data formatting | bytes 2097152 | tf_op jit(solution)/shard_map/reshape | solution.py:70
  194.7 2.7 %convolution_convert_fusion.2 = bf16[1024,512]{1,0:T(8,128)(2,1)} fusion(bf16[1024,512]{1,0:T(8,128)(2,1)S(1)} %reshape.96, bf16[512,512]{1,0:T(8,128)(2,1)} %param.15), kind=kOutput, calls=%fused_computation.50 | convolution fusion | flops 537395200 | bytes 2621440 | tf_op jit(solution)/shard_map/dot_general | solution.py:69
  197.4 2.3 reshape.97
  199.6 9.0 %all-to-all-start.1 = ((bf16[512,1,2,512]{3,2,1,0:T(2,128)(2,1)}), bf16[512,1,2,512]{3,2,1,0:T(2,128)(2,1)S(1)}, u32[]{:S(2)}, u32[]{:S(2)}) async-start(bf16[512,1,2,512]{3,2,1,0:T(2,128)(2,1)} %bitcast.83), calls=%async_computation.1 | async-start | bytes 2097152 | tf_op jit(solution)/shard_map/all_to_all | solution.py:75
  208.7 0.6 dynamic_slice.4
  209.3 0.6 iota_compare_fusion
  209.9 23.2 %all-to-all-done.1 = bf16[512,1,2,512]{3,2,1,0:T(2,128)(2,1)S(1)} async-done(((bf16[512,1,2,512]{3,2,1,0:T(2,128)(2,1)}), bf16[512,1,2,512]{3,2,1,0:T(2,128)(2,1)S(1)}, u32[]{:S(2)}, u32[]{:S(2)}) %all-to-all-start.1) | async-done | bytes 1048608 | tf_op jit(solution)/shard_map/all_to_all | solution.py:75
  233.1 0.2 copy.42
  233.3 0.3 convert_bitcast_fusion
  233.6 2.9 %copy.43 = f32[16,32,1,2,512]{4,3,1,0,2:T(2,128)} copy(f32[16,32,1,2,512]{4,0,1,3,2:T(8,128)S(1)} %convert_bitcast_fusion) | data formatting | bytes 4194304 | tf_op jit(solution)/shard_map/convert_element_type | solution.py:78
  236.5 3.7 %reshape.100 = f32[16,64,512]{2,1,0:T(8,128)} reshape(f32[16,32,1,2,512]{4,3,1,0,2:T(2,128)} %copy.43) | data formatting | bytes 4194304 | tf_op jit(solution)/shard_map/convert_element_type | solution.py:78
  240.2 2.2 fusion.18
  242.4 1.3 fusion.20
  243.7 7.8 %fusion.35 = f32[1024,512]{1,0:T(8,128)} fusion(bf16[2048,512]{1,0:T(8,128)(2,1)S(1)} %copy-done, bf16[1024,512]{1,0:T(8,128)(2,1)} %bitcast.88, bf16[512,2048]{1,0:T(8,128)(2,1)} %param.16), kind=kOutput, calls=%fused_computation.52 | convolution fusion | flops 4299161600 | bytes 7340032 | tf_op jit(solution)/shard_map/dot_general | solution.py:85
  251.5 3.0 %fusion.22 = bf16[16,64,512]{2,1,0:T(8,128)(2,1)} fusion(f32[16,64,512]{2,1,0:T(8,128)} %bitcast.85, bf16[16,64,512]{2,1,0:T(8,128)(2,1)S(1)} %get-tuple-element.6, pred[16]{0:T(512)(128)(4,1)S(1)} %iota_compare_fusion), kind=kLoop, calls=%fused_computation.38 | loop fusion | flops 2097152 | bytes 4194320 | tf_op jit(solution)/shard_map/convert_element_type | solution.py:88
  (15 shorter events, 0.1 us)
Async XLA Ops:
  0.0 243.7 %copy-start = (bf16[2048,512]{1,0:T(8,128)(2,1)S(1)}, bf16[2048,512]{1,0:T(8,128)(2,1)}, u32[]{:S(2)}) copy-start(bf16[2048,512]{1,0:T(8,128)(2,1)} %param.17) | copy-start | bytes 6291460
  0.0 4.0 %copy-start.6 = (bf16[512,1536]{1,0:T(8,128)(2,1)S(1)}, bf16[512,1536]{1,0:T(8,128)(2,1)}, u32[]{:S(2)}) copy-start(bf16[512,1536]{1,0:T(8,128)(2,1)} %param.12) | copy-start | bytes 4718596
  29.7 6.2 %copy-start.3 = (bf16[16,64,1,8,64]{1,4,3,0,2:T(8,128)(2,1)S(1)}, bf16[16,64,1,8,64]{1,4,3,0,2:T(8,128)(2,1)}, u32[]{:S(2)}) copy-start(bf16[16,64,1,8,64]{1,4,3,0,2:T(8,128)(2,1)} %copy.47) | copy-start | bytes 3145732
  35.9 1.2 copy-start.1
  35.9 1.3 copy-start.4
  38.1 1.0 copy-start.2
  38.1 1.8 copy-start.7
  56.8 12.5 %copy-start.5 = (s32[32]{0:T(128)S(1)}, s32[32]{0:T(128)}, u32[]{:S(2)}) copy-start(s32[32]{0:T(128)} %param.10) | copy-start | bytes 388
  56.8 84.0 %all-to-all-start = ((bf16[16,32,2,1536]{3,0,2,1:T(8,128)(2,1)}), bf16[16,32,2,1536]{3,0,2,1:T(8,128)(2,1)}, u32[]{:S(2)}, u32[]{:S(2)}) async-start(bf16[16,32,2,1536]{3,0,2,1:T(8,128)(2,1)} %copy.34), calls=%async_computation | async-start | bytes 6291456 | tf_op jit(solution)/shard_map/all_to_all | solution.py:55
  199.6 33.5 %all-to-all-start.1 = ((bf16[512,1,2,512]{3,2,1,0:T(2,128)(2,1)}), bf16[512,1,2,512]{3,2,1,0:T(2,128)(2,1)S(1)}, u32[]{:S(2)}, u32[]{:S(2)}) async-start(bf16[512,1,2,512]{3,2,1,0:T(2,128)(2,1)} %bitcast.83), calls=%async_computation.1 | async-start | bytes 2097152 | tf_op jit(solution)/shard_map/all_to_all | solution.py:75
where the time goes:
time: 259 us; the launch traced here: 255 us
  waiting for transfers between devices  94.5 us (36%)
  local copies, waits for them, and re-layouts  79.5 us (31%)
  matrix products  41.8 us (16%)
  starting transfers between devices  21.5 us (8%)
  other arithmetic  17.1 us (7%)
    all_to_all x1, waiting for transfers between devices, per_device(): lax.all_to_all(triples_local, 'seq', split_axis=1, concat_axis=0, tiled=T...  71.3 us
    all_to_all x1, waiting for transfers between devices, per_device(): lax.all_to_all(scene_out, 'seq', split_axis=0, concat_axis=1, tiled=True)  23.2 us
    unnamed x20, local copies, waits for them, and re-layouts  15.4 us
    reshape x2, local copies, waits for them, and re-layouts, per_device(): triples_local.astype(jnp.bfloat16)  13.4 us
    all_to_all x1, starting transfers between devices, per_device(): lax.all_to_all(triples_local, 'seq', split_axis=1, concat_axis=0, tiled=T...  12.5 us
    sub x1, matrix products, per_device(): probs = jax.nn.softmax(logits, axis=-1).astype(jnp.bfloat16)  11 us
    all_to_all x1, starting transfers between devices, per_device(): lax.all_to_all(scene_out, 'seq', split_axis=0, concat_axis=1, tiled=True)  9.02 us
    reshape x1, local copies, waits for them, and re-layouts, per_device(): packed.astype(jnp.bfloat16).reshape(agents, step_count, 3, HEADS, head_size)  8.86 us
  transfers between devices with their start and end apart: 2, of which 2 were waited for; matrix products, arithmetic and copies ran while one was open for 1% of the time, Pallas kernels for 0%

commit v1 on v0

v1 whole, which is shorter than its diff:
```python
import jax
import jax.numpy as jnp
from jax import lax
from jax.experimental import pallas as pl
from jax.experimental.pallas import tpu as pltpu
from jax.sharding import PartitionSpec as P

D = 512
FF = 2048
SLOTS = 16
STEPS = 64
GROUPS = 32
LOCAL = STEPS // GROUPS
AGENTS = SLOTS * GROUPS
LIVE = 320
GROUP = 4
ROWS = GROUP * STEPS
PAIR = 128
INV_ROOT = 0.125
BF16 = jnp.bfloat16
F32 = jnp.float32


def dot(a, b):
    return jnp.dot(a, b, preferred_element_type=F32)


def dot_nt(a, b):
    return lax.dot_general(a, b, (((1,), (1,)), ((), ())), preferred_element_type=F32)


def rms(values, gain):
    floats = values.astype(F32)
    inverse = lax.rsqrt(jnp.mean(floats * floats, axis=-1, keepdims=True) + 1e-06)
    return (floats * inverse * gain).astype(BF16)


def iota(shape, dim):
    return lax.broadcasted_iota(jnp.int32, shape, dim)


def regroup():
    row, col = iota((256, 256), 0), iota((256, 256), 1)
    return jnp.where(col == (row & 15) * 16 + (row >> 4), 1.0, 0.0).astype(BF16)


def head_split(q):
    low = iota(q.shape, 1) < 64
    q = q.astype(F32) * INV_ROOT
    first = jnp.where(low, q, 0.0)
    return jnp.concatenate([first, q - first], axis=0).astype(BF16)


def attend(scores, v):
    top = jnp.max(scores, axis=-1, keepdims=True)
    p = jnp.exp(scores - top).astype(BF16)
    both = dot(p, jnp.concatenate([v, jnp.ones_like(v)], axis=1))
    n = both.shape[0] // 2
    low = iota((n, PAIR), 1) < 64
    top_rows = both[:n]
    bottom = both[n:]
    value = jnp.where(low, top_rows[:, :PAIR], bottom[:, :PAIR])
    total = jnp.where(low, top_rows[:, PAIR:], bottom[:, PAIR:])
    return (value / total).astype(BF16)


def time_kernel(counts, tokens, gains, qkv_w, out_w, result, x1, ctx):
    step = pl.program_id(0)
    count = counts[lax.axis_index("seq")]
    first = step * GROUP

    @pl.when(first < count)
    def _():
        values = tokens[...].reshape(ROWS, D)
        packed = dot(rms(values, gains[0:1, :]), qkv_w[...]).astype(BF16)
        block = 2 * STEPS
        same = ((iota((2 * block, block), 0) >> 6) & 1) == (iota((2 * block, block), 1) >> 6)
        for pair in range(GROUP // 2):
            rows = slice(pair * block, (pair + 1) * block)
            for head in range(D // PAIR):
                low = head * PAIR
                q = packed[rows, low : low + PAIR]
                k = packed[rows, D + low : D + low + PAIR]
                v = packed[rows, 2 * D + low : 2 * D + low + PAIR]
                scores = jnp.where(same, dot_nt(head_split(q), k), -1e30)
                ctx[rows, low : low + PAIR] = attend(scores, v)
        update = dot(ctx[...], out_w[...])
        after = (values.astype(F32) + update).astype(BF16)
        x1[pl.ds(first, GROUP)] = after.reshape(GROUP, STEPS, D)

    @pl.when(first >= count)
    def _():
        x1[pl.ds(first, GROUP)] = jnp.zeros((GROUP, STEPS, D), BF16)

    @pl.when(step == SLOTS // GROUP - 1)
    def _():
        turn = regroup()
        for part in range(STEPS // 16):
            rows = x1[:, part * 16 : (part + 1) * 16, :].reshape(256, D)
            turned = dot(turn, rows).astype(BF16)
            many = 16 // LOCAL
            result[part * many : (part + 1) * many] = turned.reshape(many, LOCAL * SLOTS, D)


def time_part(counts, tokens, gains, qkv_w, out_w):
    whole = lambda *shape: pl.BlockSpec(shape, lambda i: (0,) * len(shape))
    return pl.pallas_call(
        time_kernel,
        grid=(SLOTS // GROUP,),
        in_specs=[
            pl.BlockSpec(memory_space=pltpu.SMEM),
            pl.BlockSpec((GROUP, STEPS, D), lambda i: (i, 0, 0)),
            whole(3, D),
            whole(D, 3 * D),
            whole(D, D),
        ],
        out_specs=whole(GROUPS, LOCAL * SLOTS, D),
        out_shape=jax.ShapeDtypeStruct((GROUPS, LOCAL * SLOTS, D), BF16),
        scratch_shapes=[pltpu.VMEM((SLOTS, STEPS, D), BF16), pltpu.VMEM((ROWS, D), BF16)],
        compiler_params=pltpu.CompilerParams(vmem_limit_bytes=32 << 20),
        cost_estimate=pl.CostEstimate(
            flops=6 << 30, bytes_accessed=4 << 20, transcendentals=1 << 20
        ),
        name="time_part",
    )(counts, tokens, gains, qkv_w, out_w)


def scene_kernel(
    counts, recv, gains, qkv_hbm, out_hbm, in_hbm, back_hbm, result,
    qkv_w, out_w, in_w, back_w, xs, packed, ctx, sems,
):
    sources = (qkv_hbm, out_hbm, in_hbm, back_hbm)
    copies = [
        pltpu.make_async_copy(source, target, sems.at[i])
        for i, (source, target) in enumerate(zip(sources, (qkv_w, out_w, in_w, back_w)))
    ]
    for copy in copies:
        copy.start()

    slot = iota((8, AGENTS), 1)
    inside = slot & 15
    place = jnp.full((8, AGENTS), -1, jnp.int32)
    offsets, offset = [], jnp.int32(0)
    for block in range(GROUPS):
        count = counts[block]
        here = ((slot >> 4) == block) & (inside < count)
        place = jnp.where(here, inside + offset, place)
        offsets.append((offset, count))
        offset = offset + count
    gather = jnp.where(iota((LIVE, AGENTS), 0) == place[0:1], 1.0, 0.0).astype(BF16)
    for local in range(LOCAL):
        x = recv[:, local * SLOTS : (local + 1) * SLOTS, :].reshape(AGENTS, D)
        xs[local * LIVE : (local + 1) * LIVE] = dot(gather, x).astype(BF16)

    copies[0].wait()
    for local in range(LOCAL):
        rows = slice(local * LIVE, (local + 1) * LIVE)
        packed[rows] = dot(rms(xs[rows], gains[1:2, :]), qkv_w[...]).astype(BF16)
    for local in range(LOCAL):
        rows = slice(local * LIVE, (local + 1) * LIVE)
        for head in range(D // PAIR):
            low = head * PAIR
            q = packed[rows, low : low + PAIR]
            k = packed[rows, D + low : D + low + PAIR]
            v = packed[rows, 2 * D + low : 2 * D + low + PAIR]
            ctx[rows, low : low + PAIR] = attend(dot_nt(head_split(q), k), v)
    for copy in copies[1:]:
        copy.wait()

    lane = iota((SLOTS, LIVE), 1) - iota((SLOTS, LIVE), 0)
    row = iota((SLOTS, LIVE), 0)
    scatter = jnp.concatenate(
        [
            jnp.where((lane == start) & (row < count), 1.0, 0.0).astype(BF16)
            for start, count in offsets
        ],
        axis=0,
    )
    for local in range(LOCAL):
        rows = slice(local * LIVE, (local + 1) * LIVE)
        o2 = dot(ctx[rows], out_w[...]).astype(BF16)
        x2 = (xs[rows].astype(F32) + o2.astype(F32)).astype(BF16)
        hidden = jnp.maximum(dot(rms(x2, gains[2:3, :]), in_w[...]), 0.0).astype(BF16)
        encoded = (x2.astype(F32) + dot(hidden, back_w[...])).astype(BF16)
        spread = dot(scatter, encoded).astype(BF16)
        result[:, local * SLOTS : (local + 1) * SLOTS, :] = spread.reshape(GROUPS, SLOTS, D)


def scene_part(counts, recv, gains, qkv_w, out_w, mlp_in, mlp_out):
    vmem = pl.BlockSpec(memory_space=pltpu.VMEM)
    hbm = pl.BlockSpec(memory_space=pl.ANY)
    return pl.pallas_call(
        scene_kernel,
        in_specs=[pl.BlockSpec(memory_space=pltpu.SMEM), vmem, vmem, hbm, hbm, hbm, hbm],
        out_specs=vmem,
        out_shape=jax.ShapeDtypeStruct((GROUPS, LOCAL * SLOTS, D), BF16),
        scratch_shapes=[
            pltpu.VMEM((D, 3 * D), BF16),
            pltpu.VMEM((D, D), BF16),
            pltpu.VMEM((D, FF), BF16),
            pltpu.VMEM((FF, D), BF16),
            pltpu.VMEM((LOCAL * LIVE, D), BF16),
            pltpu.VMEM((LOCAL * LIVE, 3 * D), BF16),
            pltpu.VMEM((LOCAL * LIVE, D), BF16),
            pltpu.SemaphoreType.DMA((4,)),
        ],
        compiler_params=pltpu.CompilerParams(vmem_limit_bytes=40 << 20),
        cost_estimate=pl.CostEstimate(
            flops=10 << 30, bytes_accessed=8 << 20, transcendentals=2 << 20
        ),
        name="scene_part",
    )(counts, recv, gains, qkv_w, out_w, mlp_in, mlp_out)


def order_kernel(recv, result):
    rows = recv[...].reshape(256, D)
    result[...] = dot(regroup(), rows).astype(BF16).reshape(SLOTS, 16, D)


def order_part(recv):
    many = 16 // LOCAL
    return pl.pallas_call(
        order_kernel,
        grid=(STEPS // 16,),
        in_specs=[pl.BlockSpec((many, LOCAL * SLOTS, D), lambda i: (i, 0, 0))],
        out_specs=pl.BlockSpec((SLOTS, 16, D), lambda i: (0, i, 0)),
        out_shape=jax.ShapeDtypeStruct((SLOTS, STEPS, D), BF16),
        name="order_part",
    )(recv)


def exchange(values):
    return lax.all_to_all(values, "seq", split_axis=0, concat_axis=0, tiled=True)


def per_device(
    tokens, block_counts, gains, qkv_time, out_time, qkv_scene, out_scene, mlp_in, mlp_out
):
    after_time = exchange(time_part(block_counts, tokens, gains, qkv_time, out_time))
    encoded = scene_part(block_counts, after_time, gains, qkv_scene, out_scene, mlp_in, mlp_out)
    return order_part(exchange(encoded))


def solution(mesh):
    placed = (P(("scene", "seq"), None, None), P("scene"), P(), P(), P(), P(), P(), P(), P())
    return jax.shard_map(
        per_device,
        mesh=mesh,
        in_specs=placed,
        out_specs=P(("scene", "seq"), None, None),
        check_vma=False,
    )
```

time: 259 us -> 103 us (0.40)
  the two profiles are of different devices: /device:TPU:1 before, /device:TPU:6 now
where the time goes in v1:
time: 103 us; the launch traced here: 102 us
  blocking collectives  73.2 us (71%)
  Pallas kernels  23.7 us (23%)
  local copies, waits for them, and re-layouts  5.05 us (5%)
    all_to_all x2, blocking collectives, exchange(): lax.all_to_all(values, 'seq', split_axis=0, concat_axis=0, tiled=True)  73.2 us
    pallas_call x1, Pallas kernels, scene_part(): pl.pallas_call(scene_kernel, in_specs=[pl.BlockSpec(memory_space=pltpu.SM...  10.9 us
    pallas_call x1, Pallas kernels, time_part(): pl.pallas_call(time_kernel, grid=(SLOTS // GROUP,), in_specs=[pl.BlockSpe...  9 us
    unnamed x22, local copies, waits for them, and re-layouts  5.05 us
    pallas_call x1, Pallas kernels, order_part(): pl.pallas_call(order_kernel, grid=(STEPS // 16,), in_specs=[pl.BlockSpec(...  3.77 us

profile of v1, /device:TPU:6, one launch (start us, length us, event | category | flops | bytes accessed | tf_op | source)
XLA Modules:
  0.0 102.0 jit_solution(2861072530932182797)
XLA Ops:
  0.0 0.0 copy-start.2
  0.0 1.4 %copy-done.2 = bf16[512,1536]{1,0:T(8,128)(2,1)S(1)} copy-done((bf16[512,1536]{1,0:T(8,128)(2,1)S(1)}, bf16[512,1536]{1,0:T(8,128)(2,1)}, u32[]{:S(2)}) %copy-start.2) | copy-done | bytes 1572888
  1.4 0.0 copy-start.4
  1.4 1.2 %copy-done.4 = bf16[16,64,512]{2,1,0:T(8,128)(2,1)S(1)} copy-done((bf16[16,64,512]{2,1,0:T(8,128)(2,1)S(1)}, bf16[16,64,512]{2,1,0:T(8,128)(2,1)}, u32[]{:S(2)}) %copy-start.4) | copy-done | bytes 1048600
  2.6 0.0 copy-start.5
  2.6 1.0 %copy-done.5 = bf16[512,512]{1,0:T(8,128)(2,1)S(1)} copy-done((bf16[512,512]{1,0:T(8,128)(2,1)S(1)}, bf16[512,512]{1,0:T(8,128)(2,1)}, u32[]{:S(2)}) %copy-start.5) | copy-done | bytes 524312
  3.7 0.0 copy-start.7
  3.7 0.7 copy-done.7
  4.4 0.0 copy-start.9
  4.4 0.7 copy-done.9
  5.0 0.0 copy-start.1
  5.0 0.0 copy-start.3
  5.0 0.0 copy-start.6
  5.0 0.0 copy-start.8
  5.0 0.0 copy-start.10
  5.1 9.0 %time_part.1 = bf16[32,32,512]{2,1,0:T(8,128)(2,1)S(1)} custom-call(s32[32]{0:T(128)S(1)} %copy-done.9, bf16[16,64,512]{2,1,0:T(8,128)(2,1)S(1)} %copy-done.4, f32[3,512]{1,0:T(4,128)S(1)} %copy-done.7, bf16[512,1536]{1,0:T(8,128)(2,1)S(1)} %copy-done.2, bf16[512,512]{1,0:T(8,128)(2,1)S(1)} %copy-done.5), custom_call_target="tpu_custom_call" | custom-call | flops 6442450944 | bytes 4194304 | tf_op jit(solution)/shard_map/time_part/pallas_call | solution.py:107
  14.1 0.0 copy-start
  14.1 40.0 %all_to_all.10.recv = bf16[32,32,512]{2,1,0:T(8,128)(2,1)S(1)} all-to-all(bf16[32,32,512]{2,1,0:T(8,128)(2,1)S(1)} %time_part.1), channel_id=1, replica_groups=mesh['scene'=8,'seq'=32] {'seq'}, dimensions={0} | all-to-all | bytes 2097152 | tf_op jit(solution)/shard_map/all_to_all | solution.py:233
  54.0 0.0 copy-done.1
  54.0 0.0 copy-done.3
  54.1 0.0 copy-done.6
  54.1 0.0 copy-done.8
  54.1 0.0 copy-done.10
  54.1 0.0 copy-done
  54.1 10.9 %scene_part.1 = bf16[32,32,512]{2,1,0:T(8,128)(2,1)S(1)} custom-call(s32[32]{0:T(128)S(1)} %copy-done.10, bf16[32,32,512]{2,1,0:T(8,128)(2,1)S(1)} %all_to_all.10.recv, f32[3,512]{1,0:T(4,128)S(1)} %copy-done.8, bf16[512,1536]{1,0:T(8,128)(2,1)S(1)} %copy-done.3, bf16[512,512]{1,0:T(8,128)(2,1)S(1)} %copy-done.6, bf16[512,2048]{1,0:T(8,128)(2,1)S(1)} %copy-done, ...), custom_call_target="tpu_custom_call" | custom-call | flops 10737418240 | bytes 8388608 | tf_op jit(solution)/shard_map/scene_part/pallas_call | solution.py:192
  65.0 33.2 %all_to_all.11.recv = bf16[32,32,512]{2,1,0:T(8,128)(2,1)} all-to-all(bf16[32,32,512]{2,1,0:T(8,128)(2,1)S(1)} %scene_part.1), channel_id=1, replica_groups=mesh['scene'=8,'seq'=32] {'seq'}, dimensions={0} | all-to-all | bytes 2097152 | tf_op jit(solution)/shard_map/all_to_all | solution.py:233
  98.2 3.8 %order_part.1 = bf16[16,64,512]{2,1,0:T(8,128)(2,1)} custom-call(bf16[32,32,512]{2,1,0:T(8,128)(2,1)} %all_to_all.11.recv), custom_call_target="tpu_custom_call" | custom-call | tf_op jit(solution)/shard_map/order_part/pallas_call | solution.py:222
Async XLA Ops:
  0.0 1.4 %copy-start.2 = (bf16[512,1536]{1,0:T(8,128)(2,1)S(1)}, bf16[512,1536]{1,0:T(8,128)(2,1)}, u32[]{:S(2)}) copy-start(bf16[512,1536]{1,0:T(8,128)(2,1)} %qkv_w.1) | copy-start | bytes 4718596
  1.4 1.2 %copy-start.4 = (bf16[16,64,512]{2,1,0:T(8,128)(2,1)S(1)}, bf16[16,64,512]{2,1,0:T(8,128)(2,1)}, u32[]{:S(2)}) copy-start(bf16[16,64,512]{2,1,0:T(8,128)(2,1)} %tokens.1) | copy-start | bytes 3145732
  2.6 1.0 %copy-start.5 = (bf16[512,512]{1,0:T(8,128)(2,1)S(1)}, bf16[512,512]{1,0:T(8,128)(2,1)}, u32[]{:S(2)}) copy-start(bf16[512,512]{1,0:T(8,128)(2,1)} %out_w.1) | copy-start | bytes 1572868
  3.7 0.7 copy-start.7
  4.4 0.7 copy-start.9
  5.0 49.0 %copy-start.1 = (bf16[2048,512]{1,0:T(8,128)(2,1)S(1)}, bf16[2048,512]{1,0:T(8,128)(2,1)}, u32[]{:S(2)}) copy-start(bf16[2048,512]{1,0:T(8,128)(2,1)} %back_hbm.1) | copy-start | bytes 6291460
  5.0 49.0 %copy-start.3 = (bf16[512,1536]{1,0:T(8,128)(2,1)S(1)}, bf16[512,1536]{1,0:T(8,128)(2,1)}, u32[]{:S(2)}) copy-start(bf16[512,1536]{1,0:T(8,128)(2,1)} %qkv_hbm.1) | copy-start | bytes 4718596
  5.0 49.0 %copy-start.6 = (bf16[512,512]{1,0:T(8,128)(2,1)S(1)}, bf16[512,512]{1,0:T(8,128)(2,1)}, u32[]{:S(2)}) copy-start(bf16[512,512]{1,0:T(8,128)(2,1)} %out_hbm.1) | copy-start | bytes 1572868
  5.0 49.0 %copy-start.8 = (f32[3,512]{1,0:T(4,128)S(1)}, f32[3,512]{1,0:T(4,128)}, u32[]{:S(2)}) copy-start(f32[3,512]{1,0:T(4,128)} %gains.3) | copy-start | bytes 18436
  5.0 49.0 %copy-start.10 = (s32[32]{0:T(128)S(1)}, s32[32]{0:T(128)}, u32[]{:S(2)}) copy-start(s32[32]{0:T(128)} %counts.3) | copy-start | bytes 388
  14.1 40.0 %copy-start = (bf16[512,2048]{1,0:T(8,128)(2,1)S(1)}, bf16[512,2048]{1,0:T(8,128)(2,1)}, u32[]{:S(2)}) copy-start(bf16[512,2048]{1,0:T(8,128)(2,1)} %in_hbm.1) | copy-start | bytes 6291460

commit v2 on v1

v2 whole, which is shorter than its diff:
```python
import jax
import jax.numpy as jnp
from jax import lax
from jax.experimental import pallas as pl
from jax.experimental.pallas import tpu as pltpu
from jax.sharding import PartitionSpec as P

D = 512
FF = 2048
SLOTS = 16
STEPS = 64
GROUPS = 32
LOCAL = STEPS // GROUPS
AGENTS = SLOTS * GROUPS
LIVE = 320
GROUP = 8
ROWS = GROUP * STEPS
QUAD = 256
LANES = 128
LOWEST = -3e38
INV_ROOT = 0.125
CUTS = 4
BF16 = jnp.bfloat16
F32 = jnp.float32


def dot(a, b):
    return jnp.dot(a, b, preferred_element_type=F32)


def dot_nt(a, b):
    return lax.dot_general(a, b, (((1,), (1,)), ((), ())), preferred_element_type=F32)


def rms(values, gain):
    floats = values.astype(F32)
    inverse = lax.rsqrt(jnp.mean(floats * floats, axis=-1, keepdims=True) + 1e-06)
    return (floats * inverse * gain).astype(BF16)


def iota(shape, dim):
    return lax.broadcasted_iota(jnp.int32, shape, dim)


def regroup():
    row, col = iota((256, 256), 0), iota((256, 256), 1)
    return jnp.where(col == (row & 15) * 16 + (row >> 4), 1.0, 0.0).astype(BF16)


def quad_masks(k):
    lane = iota(k.shape, 1) >> 6
    return jnp.concatenate([jnp.where(lane == h, k, jnp.zeros_like(k)) for h in range(4)], axis=0)


def time_group(values, gains, qkv_w, out_w, ctx):
    packed = dot(rms(values, gains[0:1, :]), qkv_w[...]).astype(BF16)
    ones = quad_masks(jnp.ones((STEPS, QUAD), BF16))
    for agent in range(GROUP):
        rows = slice(agent * STEPS, (agent + 1) * STEPS)
        for low in range(0, D, QUAD):
            q = packed[rows, low : low + QUAD] * jnp.asarray(INV_ROOT, BF16)
            k = packed[rows, D + low : D + low + QUAD]
            v = packed[rows, 2 * D + low : 2 * D + low + QUAD]
            scores = dot_nt(q, quad_masks(k))
            p = []
            for half in range(0, QUAD, LANES):
                part = scores[:, half : half + LANES]
                left = iota(part.shape, 1) < STEPS
                top0 = jnp.max(jnp.where(left, part, LOWEST), axis=-1, keepdims=True)
                top1 = jnp.max(jnp.where(left, LOWEST, part), axis=-1, keepdims=True)
                p.append(jnp.exp(part - jnp.where(left, top0, top1)))
            p = jnp.concatenate(p, axis=1).astype(BF16)
            both = dot(p, jnp.concatenate([quad_masks(v), ones], axis=1))
            ctx[rows, low : low + QUAD] = (both[:, :QUAD] / both[:, QUAD:]).astype(BF16)
    update = dot(ctx[...], out_w[...])
    return (values.astype(F32) + update).astype(BF16)


def scene_quad(q, k, v):
    scores = dot_nt(q * jnp.asarray(INV_ROOT, BF16), quad_masks(k))
    p, inverse = [], []
    for low in range(0, 4 * LIVE, 2 * LIVE):
        a = scores[:, low : low + 256]
        m = scores[:, low + 256 : low + 384]
        b = scores[:, low + 384 : low + 640]
        left = iota(m.shape, 1) < 64
        top0 = jnp.maximum(a[:, :LANES], a[:, LANES:])
        top0 = jnp.max(jnp.maximum(top0, jnp.where(left, m, LOWEST)), axis=-1, keepdims=True)
        top1 = jnp.maximum(b[:, :LANES], b[:, LANES:])
        top1 = jnp.max(jnp.maximum(top1, jnp.where(left, LOWEST, m)), axis=-1, keepdims=True)
        a, b = jnp.exp(a - top0), jnp.exp(b - top1)
        m = jnp.exp(m - jnp.where(left, top0, top1))
        sum0 = a[:, :LANES] + a[:, LANES:] + jnp.where(left, m, 0.0)
        sum1 = b[:, :LANES] + b[:, LANES:] + jnp.where(left, 0.0, m)
        sum0 = jnp.sum(sum0, axis=-1, keepdims=True)
        sum1 = jnp.sum(sum1, axis=-1, keepdims=True)
        p += [a.astype(BF16), m.astype(BF16), b.astype(BF16)]
        inverse.append(1.0 / jnp.where(left, sum0, sum1))
    value = dot(jnp.concatenate(p, axis=1), quad_masks(v))
    return (value * jnp.concatenate(inverse, axis=1)).astype(BF16)


def time_kernel(
    counts, tokens_hbm, gains, qkv_hbm, out_hbm, result, tokens, qkv_w, out_w, x1, ctx, sems
):
    many = SLOTS // GROUP
    cut = D // CUTS

    def tokens_copy(i):
        part = pl.ds(pl.multiple_of(i * GROUP, GROUP), GROUP)
        return pltpu.make_async_copy(tokens_hbm.at[part], tokens.at[part], sems.at[i])

    def weight_copies(source, target, first):
        parts = [pl.ds(i * cut, cut) for i in range(CUTS)]
        return [
            pltpu.make_async_copy(source.at[part], target.at[part], sems.at[first + i])
            for i, part in enumerate(parts)
        ]

    tokens_copy(0).start()
    weights = weight_copies(qkv_hbm, qkv_w, many) + weight_copies(out_hbm, out_w, many + CUTS)
    for copy in weights:
        copy.start()
    for i in range(1, many):
        tokens_copy(i).start()
    count = counts[lax.axis_index("seq")]
    for copy in weights[:CUTS]:
        copy.wait()

    def group(i, _):
        first = pl.multiple_of(i * GROUP, GROUP)
        tokens_copy(i).wait()

        @pl.when(i == 0)
        def _():
            for copy in weights[CUTS:]:
                copy.wait()

        @pl.when(first < count)
        def _():
            values = tokens[pl.ds(first, GROUP)].reshape(ROWS, D)
            after = time_group(values, gains, qkv_w, out_w, ctx)
            x1[pl.ds(first, GROUP)] = after.reshape(GROUP, STEPS, D)

        @pl.when(first >= count)
        def _():
            x1[pl.ds(first, GROUP)] = jnp.zeros((GROUP, STEPS, D), BF16)

        return 0

    lax.fori_loop(0, many, group, 0)
    turn = regroup()
    for part in range(STEPS // 16):
        rows = x1[:, part * 16 : (part + 1) * 16, :].reshape(256, D)
        turned = dot(turn, rows).astype(BF16)
        span = 16 // LOCAL
        result[part * span : (part + 1) * span] = turned.reshape(span, LOCAL * SLOTS, D)


def time_part(counts, tokens, gains, qkv_w, out_w):
    vmem = pl.BlockSpec(memory_space=pltpu.VMEM)
    hbm = pl.BlockSpec(memory_space=pltpu.HBM)
    return pl.pallas_call(
        time_kernel,
        in_specs=[pl.BlockSpec(memory_space=pltpu.SMEM), hbm, vmem, hbm, hbm],
        out_specs=vmem,
        out_shape=jax.ShapeDtypeStruct((GROUPS, LOCAL * SLOTS, D), BF16),
        scratch_shapes=[
            pltpu.VMEM((SLOTS, STEPS, D), BF16),
            pltpu.VMEM((D, 3 * D), BF16),
            pltpu.VMEM((D, D), BF16),
            pltpu.VMEM((SLOTS, STEPS, D), BF16),
            pltpu.VMEM((ROWS, D), BF16),
            pltpu.SemaphoreType.DMA((SLOTS // GROUP + 2 * CUTS,)),
        ],
        compiler_params=pltpu.CompilerParams(vmem_limit_bytes=32 << 20),
        cost_estimate=pl.CostEstimate(
            flops=6 << 30, bytes_accessed=4 << 20, transcendentals=1 << 20
        ),
        name="time_part",
    )(counts, tokens, gains, qkv_w, out_w)


def scene_kernel(
    counts, recv, gains, qkv_w, out_w, in_w, back_w, result, xs, packed, ctx
):
    slot = iota((8, AGENTS), 1)
    inside = slot & 15
    place = jnp.full((8, AGENTS), -1, jnp.int32)
    offsets, offset = [], jnp.int32(0)
    for block in range(GROUPS):
        count = counts[block]
        here = ((slot >> 4) == block) & (inside < count)
        place = jnp.where(here, inside + offset, place)
        offsets.append((offset, count))
        offset = offset + count
    gather = jnp.where(iota((LIVE, AGENTS), 0) == place[0:1], 1.0, 0.0).astype(BF16)
    for local in range(LOCAL):
        x = recv[:, local * SLOTS : (local + 1) * SLOTS, :].reshape(AGENTS, D)
        xs[local * LIVE : (local + 1) * LIVE] = dot(gather, x).astype(BF16)

    blocks = [slice(i * LIVE, (i + 1) * LIVE) for i in range(LOCAL)]
    for rows in blocks:
        packed[rows] = dot(rms(xs[rows], gains[1:2, :]), qkv_w[...]).astype(BF16)
    for rows in blocks:
        for low in range(0, D, QUAD):
            q = packed[rows, low : low + QUAD]
            k = packed[rows, D + low : D + low + QUAD]
            v = packed[rows, 2 * D + low : 2 * D + low + QUAD]
            ctx[rows, low : low + QUAD] = scene_quad(q, k, v)

    lane = iota((SLOTS, LIVE), 1) - iota((SLOTS, LIVE), 0)
    row = iota((SLOTS, LIVE), 0)
    scatter = jnp.concatenate(
        [
            jnp.where((lane == start) & (row < count), 1.0, 0.0).astype(BF16)
            for start, count in offsets
        ],
        axis=0,
    )
    for i, rows in enumerate(blocks):
        o2 = dot(ctx[rows], out_w[...]).astype(BF16)
        x2 = (xs[rows].astype(F32) + o2.astype(F32)).astype(BF16)
        hidden = jnp.maximum(dot(rms(x2, gains[2:3, :]), in_w[...]), 0.0).astype(BF16)
        encoded = (x2.astype(F32) + dot(hidden, back_w[...])).astype(BF16)
        spread = dot(scatter, encoded).astype(BF16)
        result[:, i * SLOTS : (i + 1) * SLOTS, :] = spread.reshape(GROUPS, SLOTS, D)


def scene_part(counts, recv, gains, qkv_w, out_w, mlp_in, mlp_out):
    vmem = pl.BlockSpec(memory_space=pltpu.VMEM)
    return pl.pallas_call(
        scene_kernel,
        in_specs=[pl.BlockSpec(memory_space=pltpu.SMEM)] + [vmem] * 6,
        out_specs=vmem,
        out_shape=jax.ShapeDtypeStruct((GROUPS, LOCAL * SLOTS, D), BF16),
        scratch_shapes=[
            pltpu.VMEM((LOCAL * LIVE, D), BF16),
            pltpu.VMEM((LOCAL * LIVE, 3 * D), BF16),
            pltpu.VMEM((LOCAL * LIVE, D), BF16),
        ],
        compiler_params=pltpu.CompilerParams(vmem_limit_bytes=40 << 20),
        cost_estimate=pl.CostEstimate(
            flops=10 << 30, bytes_accessed=8 << 20, transcendentals=2 << 20
        ),
        name="scene_part",
    )(counts, recv, gains, qkv_w, out_w, mlp_in, mlp_out)


def order_kernel(recv, result, turned, sems):
    turn = regroup()
    span = 16 // LOCAL
    copies = []
    for part in range(STEPS // 16):
        rows = recv[part * span : (part + 1) * span].reshape(256, D)
        turned[part] = dot(turn, rows).astype(BF16).reshape(SLOTS, 16, D)
        copies.append(
            pltpu.make_async_copy(
                turned.at[part], result.at[:, pl.ds(part * 16, 16), :], sems.at[part]
            )
        )
        copies[-1].start()
    for copy in copies:
        copy.wait()


def order_part(recv):
    return pl.pallas_call(
        order_kernel,
        in_specs=[pl.BlockSpec(memory_space=pltpu.VMEM)],
        out_specs=pl.BlockSpec(memory_space=pltpu.HBM),
        out_shape=jax.ShapeDtypeStruct((SLOTS, STEPS, D), BF16),
        scratch_shapes=[
            pltpu.VMEM((STEPS // 16, SLOTS, 16, D), BF16),
            pltpu.SemaphoreType.DMA((STEPS // 16,)),
        ],
        compiler_params=pltpu.CompilerParams(vmem_limit_bytes=16 << 20),
        name="order_part",
    )(recv)


def exchange(values):
    return lax.all_to_all(values, "seq", split_axis=0, concat_axis=0, tiled=True)


def per_device(
    tokens, block_counts, gains, qkv_time, out_time, qkv_scene, out_scene, mlp_in, mlp_out
):
    after_time = exchange(time_part(block_counts, tokens, gains, qkv_time, out_time))
    encoded = scene_part(block_counts, after_time, gains, qkv_scene, out_scene, mlp_in, mlp_out)
    return order_part(exchange(encoded))


def solution(mesh):
    placed = (P(("scene", "seq"), None, None), P("scene"), P(), P(), P(), P(), P(), P(), P())
    return jax.shard_map(
        per_device,
        mesh=mesh,
        in_specs=placed,
        out_specs=P(("scene", "seq"), None, None),
        check_vma=False,
    )
```

time: 103 us -> 97 us (0.942)
  Pallas kernels: 23.7 us -> 15.4 us
  blocking collectives: 73.2 us -> 76.1 us
    pallas_call x2, Pallas kernels: 12.8 us -> 6.8 us  [the longest x1 5.57 us: time_part(): pl.pallas_call(time_kernel, in_specs=[pl.BlockSpec(memory_space=pltpu.SME...]
    all_to_all x2, blocking collectives: 73.2 us -> 76.1 us  [exchange(): lax.all_to_all(values, 'seq', split_axis=0, concat_axis=0, tiled=True)]
    pallas_call x1, Pallas kernels: 10.9 us -> 8.59 us  [scene_part(): pl.pallas_call(scene_kernel, in_specs=[pl.BlockSpec(memory_space=pltpu.SM...]
where the time goes in v2:
time: 97 us; the launch traced here: 96.6 us
  blocking collectives  76.1 us (78%)
  Pallas kernels  15.4 us (16%)
  local copies, waits for them, and re-layouts  5.05 us (5%)
    all_to_all x2, blocking collectives, exchange(): lax.all_to_all(values, 'seq', split_axis=0, concat_axis=0, tiled=True)  76.1 us
    pallas_call x1, Pallas kernels, scene_part(): pl.pallas_call(scene_kernel, in_specs=[pl.BlockSpec(memory_space=pltpu.SM...  8.59 us
    pallas_call x1, Pallas kernels, time_part(): pl.pallas_call(time_kernel, in_specs=[pl.BlockSpec(memory_space=pltpu.SME...  5.57 us
    unnamed x22, local copies, waits for them, and re-layouts  5.05 us

profile of v2, /device:TPU:6, one launch (start us, length us, event | category | flops | bytes accessed | tf_op | source)
XLA Modules:
  0.0 96.6 jit_solution(10053652002432720832)
XLA Ops:
  0.0 0.0 copy-start.2
  0.0 1.4 %copy-done.2 = bf16[512,1536]{1,0:T(8,128)(2,1)S(1)} copy-done((bf16[512,1536]{1,0:T(8,128)(2,1)S(1)}, bf16[512,1536]{1,0:T(8,128)(2,1)}, u32[]{:S(2)}) %copy-start.2) | copy-done | bytes 1572888
  1.4 0.0 copy-start.4
  1.4 1.2 %copy-done.4 = bf16[16,64,512]{2,1,0:T(8,128)(2,1)S(1)} copy-done((bf16[16,64,512]{2,1,0:T(8,128)(2,1)S(1)}, bf16[16,64,512]{2,1,0:T(8,128)(2,1)}, u32[]{:S(2)}) %copy-start.4) | copy-done | bytes 1048600
  2.6 0.0 copy-start.5
  2.6 1.0 %copy-done.5 = bf16[512,512]{1,0:T(8,128)(2,1)S(1)} copy-done((bf16[512,512]{1,0:T(8,128)(2,1)S(1)}, bf16[512,512]{1,0:T(8,128)(2,1)}, u32[]{:S(2)}) %copy-start.5) | copy-done | bytes 524312
  3.7 0.0 copy-start.7
  3.7 0.7 copy-done.7
  4.4 0.0 copy-start.9
  4.4 0.7 copy-done.9
  5.0 0.0 copy-start.1
  5.0 0.0 copy-start.3
  5.0 0.0 copy-start.6
  5.0 0.0 copy-start.8
  5.0 0.0 copy-start.10
  5.1 5.6 %time_part.1 = bf16[32,32,512]{2,1,0:T(8,128)(2,1)S(1)} custom-call(s32[32]{0:T(128)S(1)} %copy-done.9, bf16[16,64,512]{2,1,0:T(8,128)(2,1)S(1)} %copy-done.4, f32[3,512]{1,0:T(4,128)S(1)} %copy-done.7, bf16[512,1536]{1,0:T(8,128)(2,1)S(1)} %copy-done.2, bf16[512,512]{1,0:T(8,128)(2,1)S(1)} %copy-done.5), custom_call_target="tpu_custom_call" | custom-call | flops 6442450944 | bytes 4194304 | tf_op jit(solution)/shard_map/time_part/pallas_call | solution.py:163
  10.6 0.0 copy-start
  10.6 42.9 %all_to_all.10.recv = bf16[32,32,512]{2,1,0:T(8,128)(2,1)S(1)} all-to-all(bf16[32,32,512]{2,1,0:T(8,128)(2,1)S(1)} %time_part.1), channel_id=1, replica_groups=mesh['scene'=8,'seq'=32] {'seq'}, dimensions={0} | all-to-all | bytes 2097152 | tf_op jit(solution)/shard_map/all_to_all | solution.py:283
  53.6 0.0 copy-done.1
  53.6 0.0 copy-done.3
  53.6 0.0 copy-done.6
  53.6 0.0 copy-done.8
  53.6 0.0 copy-done.10
  53.6 0.0 copy-done
  53.6 8.6 %scene_part.1 = bf16[32,32,512]{2,1,0:T(8,128)(2,1)S(1)} custom-call(s32[32]{0:T(128)S(1)} %copy-done.10, bf16[32,32,512]{2,1,0:T(8,128)(2,1)S(1)} %all_to_all.10.recv, f32[3,512]{1,0:T(4,128)S(1)} %copy-done.8, bf16[512,1536]{1,0:T(8,128)(2,1)S(1)} %copy-done.3, bf16[512,512]{1,0:T(8,128)(2,1)S(1)} %copy-done.6, bf16[512,2048]{1,0:T(8,128)(2,1)S(1)} %copy-done, ...), custom_call_target="tpu_custom_call" | custom-call | flops 10737418240 | bytes 8388608 | tf_op jit(solution)/shard_map/scene_part/pallas_call | solution.py:232
  62.2 33.2 %all_to_all.11.recv = bf16[32,32,512]{2,1,0:T(8,128)(2,1)S(1)} all-to-all(bf16[32,32,512]{2,1,0:T(8,128)(2,1)S(1)} %scene_part.1), channel_id=1, replica_groups=mesh['scene'=8,'seq'=32] {'seq'}, dimensions={0} | all-to-all | bytes 2097152 | tf_op jit(solution)/shard_map/all_to_all | solution.py:283
  95.4 1.2 %order_part.1 = bf16[16,64,512]{2,1,0:T(8,128)(2,1)} custom-call(bf16[32,32,512]{2,1,0:T(8,128)(2,1)S(1)} %all_to_all.11.recv), custom_call_target="tpu_custom_call" | custom-call | tf_op jit(solution)/shard_map/order_part/pallas_call | solution.py:268
Async XLA Ops:
  0.0 1.4 %copy-start.2 = (bf16[512,1536]{1,0:T(8,128)(2,1)S(1)}, bf16[512,1536]{1,0:T(8,128)(2,1)}, u32[]{:S(2)}) copy-start(bf16[512,1536]{1,0:T(8,128)(2,1)} %qkv_hbm.1) | copy-start | bytes 4718596
  1.4 1.2 %copy-start.4 = (bf16[16,64,512]{2,1,0:T(8,128)(2,1)S(1)}, bf16[16,64,512]{2,1,0:T(8,128)(2,1)}, u32[]{:S(2)}) copy-start(bf16[16,64,512]{2,1,0:T(8,128)(2,1)} %tokens_hbm.1) | copy-start | bytes 3145732
  2.6 1.0 %copy-start.5 = (bf16[512,512]{1,0:T(8,128)(2,1)S(1)}, bf16[512,512]{1,0:T(8,128)(2,1)}, u32[]{:S(2)}) copy-start(bf16[512,512]{1,0:T(8,128)(2,1)} %out_hbm.1) | copy-start | bytes 1572868
  3.7 0.7 copy-start.7
  4.4 0.7 copy-start.9
  5.0 48.5 %copy-start.1 = (bf16[2048,512]{1,0:T(8,128)(2,1)S(1)}, bf16[2048,512]{1,0:T(8,128)(2,1)}, u32[]{:S(2)}) copy-start(bf16[2048,512]{1,0:T(8,128)(2,1)} %back_w.1) | copy-start | bytes 6291460
  5.0 48.5 %copy-start.3 = (bf16[512,1536]{1,0:T(8,128)(2,1)S(1)}, bf16[512,1536]{1,0:T(8,128)(2,1)}, u32[]{:S(2)}) copy-start(bf16[512,1536]{1,0:T(8,128)(2,1)} %qkv_w.1) | copy-start | bytes 4718596
  5.0 48.5 %copy-start.6 = (bf16[512,512]{1,0:T(8,128)(2,1)S(1)}, bf16[512,512]{1,0:T(8,128)(2,1)}, u32[]{:S(2)}) copy-start(bf16[512,512]{1,0:T(8,128)(2,1)} %out_w.1) | copy-start | bytes 1572868
  5.0 48.5 %copy-start.8 = (f32[3,512]{1,0:T(4,128)S(1)}, f32[3,512]{1,0:T(4,128)}, u32[]{:S(2)}) copy-start(f32[3,512]{1,0:T(4,128)} %gains.3) | copy-start | bytes 18436
  5.0 48.5 %copy-start.10 = (s32[32]{0:T(128)S(1)}, s32[32]{0:T(128)}, u32[]{:S(2)}) copy-start(s32[32]{0:T(128)} %counts.3) | copy-start | bytes 388
  10.6 43.0 %copy-start = (bf16[512,2048]{1,0:T(8,128)(2,1)S(1)}, bf16[512,2048]{1,0:T(8,128)(2,1)}, u32[]{:S(2)}) copy-start(bf16[512,2048]{1,0:T(8,128)(2,1)} %in_w.1) | copy-start | bytes 6291460

commit v3 on v2

--- a/solution.py
+++ b/solution.py
@@ -178,7 +178,7 @@
             flops=6 << 30, bytes_accessed=4 << 20, transcendentals=1 << 20
         ),
         name="time_part",
-    )(counts, tokens, gains, qkv_w, out_w)
+    )(*(pltpu.with_memory_space_constraint(x, pltpu.HBM) for x in (counts, tokens, gains, qkv_w, out_w)))
 
 
 def scene_kernel(
@@ -286,8 +286,12 @@
 def per_device(
     tokens, block_counts, gains, qkv_time, out_time, qkv_scene, out_scene, mlp_in, mlp_out
 ):
-    after_time = exchange(time_part(block_counts, tokens, gains, qkv_time, out_time))
-    encoded = scene_part(block_counts, after_time, gains, qkv_scene, out_scene, mlp_in, mlp_out)
+    after_time = time_part(block_counts, tokens, gains, qkv_time, out_time)
+    after_time, *rest = lax.optimization_barrier(
+        (after_time, block_counts, gains, qkv_scene, out_scene, mlp_in, mlp_out)
+    )
+    counts, *rest = rest
+    encoded = scene_part(counts, exchange(after_time), *rest)
     return order_part(exchange(encoded))
 
 

time: 97 us -> 92.7 us (0.956)
  the two profiles are of different devices: /device:TPU:6 before, /device:TPU:2 now
where the time goes in v3:
time: 92.7 us; the launch traced here: 92.5 us
  blocking collectives  73.2 us (79%)
  Pallas kernels  19.2 us (21%)
    all_to_all x2, blocking collectives, exchange(): lax.all_to_all(values, 'seq', split_axis=0, concat_axis=0, tiled=True)  73.2 us
    pallas_call x1, Pallas kernels, time_part(): pl.pallas_call(time_kernel, in_specs=[pl.BlockSpec(memory_space=pltpu.SME...  9.35 us
    pallas_call x1, Pallas kernels, scene_part(): pl.pallas_call(scene_kernel, in_specs=[pl.BlockSpec(memory_space=pltpu.SM...  8.59 us

profile of v3, /device:TPU:2, one launch (start us, length us, event | category | flops | bytes accessed | tf_op | source)
XLA Modules:
  0.0 92.5 jit_solution(9712357507577332006)
XLA Ops:
  0.0 0.0 copy-start.1
  0.0 0.0 copy-start.2
  0.0 0.0 copy-start.3
  0.0 0.0 copy-start.4
  0.0 0.0 copy-start.5
  0.0 9.3 %time_part.1 = bf16[32,32,512]{2,1,0:T(8,128)(2,1)S(1)} custom-call(s32[32]{0:T(128)} %counts.2, bf16[16,64,512]{2,1,0:T(8,128)(2,1)} %tokens_hbm.1, f32[3,512]{1,0:T(4,128)} %gains.2, bf16[512,1536]{1,0:T(8,128)(2,1)} %qkv_hbm.1, bf16[512,512]{1,0:T(8,128)(2,1)} %out_hbm.1), custom_call_target="tpu_custom_call" | custom-call | flops 6442450944 | bytes 4194304 | tf_op jit(solution)/shard_map/time_part/pallas_call | solution.py:163
  9.4 0.0 copy-start
  9.4 40.0 %all_to_all.10.recv = bf16[32,32,512]{2,1,0:T(8,128)(2,1)S(1)} all-to-all(bf16[32,32,512]{2,1,0:T(8,128)(2,1)S(1)} %time_part.1), channel_id=1, replica_groups=mesh['scene'=8,'seq'=32] {'seq'}, dimensions={0} | all-to-all | bytes 2097152 | tf_op jit(solution)/shard_map/all_to_all | solution.py:283
  49.4 0.0 copy-done.1
  49.4 0.0 copy-done.2
  49.4 0.0 copy-done.3
  49.4 0.0 copy-done.4
  49.5 0.0 copy-done.5
  49.5 0.0 copy-done
  49.5 8.6 %scene_part.1 = bf16[32,32,512]{2,1,0:T(8,128)(2,1)S(1)} custom-call(s32[32]{0:T(128)S(1)} %copy-done.5, bf16[32,32,512]{2,1,0:T(8,128)(2,1)S(1)} %all_to_all.10.recv, f32[3,512]{1,0:T(4,128)S(1)} %copy-done.4, bf16[512,1536]{1,0:T(8,128)(2,1)S(1)} %copy-done.2, bf16[512,512]{1,0:T(8,128)(2,1)S(1)} %copy-done.3, bf16[512,2048]{1,0:T(8,128)(2,1)S(1)} %copy-done, ...), custom_call_target="tpu_custom_call" | custom-call | flops 10737418240 | bytes 8388608 | tf_op jit(solution)/shard_map/scene_part/pallas_call | solution.py:232
  58.1 33.2 %all_to_all.11.recv = bf16[32,32,512]{2,1,0:T(8,128)(2,1)S(1)} all-to-all(bf16[32,32,512]{2,1,0:T(8,128)(2,1)S(1)} %scene_part.1), channel_id=1, replica_groups=mesh['scene'=8,'seq'=32] {'seq'}, dimensions={0} | all-to-all | bytes 2097152 | tf_op jit(solution)/shard_map/all_to_all | solution.py:283
  91.3 1.2 %order_part.1 = bf16[16,64,512]{2,1,0:T(8,128)(2,1)} custom-call(bf16[32,32,512]{2,1,0:T(8,128)(2,1)S(1)} %all_to_all.11.recv), custom_call_target="tpu_custom_call" | custom-call | tf_op jit(solution)/shard_map/order_part/pallas_call | solution.py:268
Async XLA Ops:
  0.0 49.4 %copy-start.1 = (bf16[2048,512]{1,0:T(8,128)(2,1)S(1)}, bf16[2048,512]{1,0:T(8,128)(2,1)}, u32[]{:S(2)}) copy-start(bf16[2048,512]{1,0:T(8,128)(2,1)} %back_w) | copy-start | bytes 6291460
  0.0 49.4 %copy-start.2 = (bf16[512,1536]{1,0:T(8,128)(2,1)S(1)}, bf16[512,1536]{1,0:T(8,128)(2,1)}, u32[]{:S(2)}) copy-start(bf16[512,1536]{1,0:T(8,128)(2,1)} %qkv_w) | copy-start | bytes 4718596
  0.0 49.4 %copy-start.3 = (bf16[512,512]{1,0:T(8,128)(2,1)S(1)}, bf16[512,512]{1,0:T(8,128)(2,1)}, u32[]{:S(2)}) copy-start(bf16[512,512]{1,0:T(8,128)(2,1)} %out_w) | copy-start | bytes 1572868
  0.0 49.4 %copy-start.4 = (f32[3,512]{1,0:T(4,128)S(1)}, f32[3,512]{1,0:T(4,128)}, u32[]{:S(2)}) copy-start(f32[3,512]{1,0:T(4,128)} %gains.2) | copy-start | bytes 18436
  0.0 49.4 %copy-start.5 = (s32[32]{0:T(128)S(1)}, s32[32]{0:T(128)}, u32[]{:S(2)}) copy-start(s32[32]{0:T(128)} %counts.2) | copy-start | bytes 388
  9.4 40.1 %copy-start = (bf16[512,2048]{1,0:T(8,128)(2,1)S(1)}, bf16[512,2048]{1,0:T(8,128)(2,1)}, u32[]{:S(2)}) copy-start(bf16[512,2048]{1,0:T(8,128)(2,1)} %in_w) | copy-start | bytes 6291460

commit v4 on v2

--- a/solution.py
+++ b/solution.py
@@ -1,3 +1,5 @@
+import functools
+
 import jax
 import jax.numpy as jnp
 from jax import lax
@@ -13,12 +15,12 @@
 LOCAL = STEPS // GROUPS
 AGENTS = SLOTS * GROUPS
 LIVE = 320
-GROUP = 8
-ROWS = GROUP * STEPS
 QUAD = 256
 LANES = 128
 LOWEST = -3e38
 INV_ROOT = 0.125
+EARLY = 4
+LATE_SIZE = 4
 CUTS = 4
 BF16 = jnp.bfloat16
 F32 = jnp.float32
@@ -42,9 +44,10 @@
     return lax.broadcasted_iota(jnp.int32, shape, dim)
 
 
-def regroup():
-    row, col = iota((256, 256), 0), iota((256, 256), 1)
-    return jnp.where(col == (row & 15) * 16 + (row >> 4), 1.0, 0.0).astype(BF16)
+def regroup(slots):
+    size = (slots * 16, slots * 16)
+    row, col = iota(size, 0), iota(size, 1)
+    return jnp.where(row == (col & 15) * slots + (col >> 4), 1.0, 0.0).astype(BF16)
 
 
 def quad_masks(k):
@@ -53,9 +56,10 @@
 
 
 def time_group(values, gains, qkv_w, out_w, ctx):
+    agents = values.shape[0] // STEPS
     packed = dot(rms(values, gains[0:1, :]), qkv_w[...]).astype(BF16)
     ones = quad_masks(jnp.ones((STEPS, QUAD), BF16))
-    for agent in range(GROUP):
+    for agent in range(agents):
         rows = slice(agent * STEPS, (agent + 1) * STEPS)
         for low in range(0, D, QUAD):
             q = packed[rows, low : low + QUAD] * jnp.asarray(INV_ROOT, BF16)
@@ -100,15 +104,17 @@
     return (value * jnp.concatenate(inverse, axis=1)).astype(BF16)
 
 
-def time_kernel(
-    counts, tokens_hbm, gains, qkv_hbm, out_hbm, result, tokens, qkv_w, out_w, x1, ctx, sems
-):
-    many = SLOTS // GROUP
+def time_kernel(base, size, extra, counts, tokens_hbm, gains, qkv_hbm, out_hbm, *refs):
+    later_hbm, (result, *later) = refs[:extra], refs[extra : 2 * extra + 1]
+    tokens, qkv_w, out_w, x1, ctx, sems, later_sems = refs[2 * extra + 1 :]
+    slots = tokens.shape[0]
+    many = slots // size
     cut = D // CUTS
 
     def tokens_copy(i):
-        part = pl.ds(pl.multiple_of(i * GROUP, GROUP), GROUP)
-        return pltpu.make_async_copy(tokens_hbm.at[part], tokens.at[part], sems.at[i])
+        first = pl.multiple_of(i * size, size)
+        source = tokens_hbm.at[pl.ds(base + first, size)]
+        return pltpu.make_async_copy(source, tokens.at[pl.ds(first, size)], sems.at[i])
 
     def weight_copies(source, target, first):
         parts = [pl.ds(i * cut, cut) for i in range(CUTS)]
@@ -126,9 +132,15 @@
     count = counts[lax.axis_index("seq")]
     for copy in weights[:CUTS]:
         copy.wait()
+    fetches = [
+        pltpu.make_async_copy(source, target, later_sems.at[i])
+        for i, (source, target) in enumerate(zip(later_hbm, later))
+    ]
+    for fetch in fetches:
+        fetch.start()
 
     def group(i, _):
-        first = pl.multiple_of(i * GROUP, GROUP)
+        first = pl.multiple_of(i * size, size)
         tokens_copy(i).wait()
 
         @pl.when(i == 0)
@@ -136,68 +148,109 @@
             for copy in weights[CUTS:]:
                 copy.wait()
 
-        @pl.when(first < count)
+        @pl.when(base + first < count)
         def _():
-            values = tokens[pl.ds(first, GROUP)].reshape(ROWS, D)
+            values = tokens[pl.ds(first, size)].reshape(size * STEPS, D)
             after = time_group(values, gains, qkv_w, out_w, ctx)
-            x1[pl.ds(first, GROUP)] = after.reshape(GROUP, STEPS, D)
-
-        @pl.when(first >= count)
+            x1[pl.ds(first, size)] = after.reshape(size, STEPS, D)
+
+        @pl.when(base + first >= count)
         def _():
-            x1[pl.ds(first, GROUP)] = jnp.zeros((GROUP, STEPS, D), BF16)
+            x1[pl.ds(first, size)] = jnp.zeros((size, STEPS, D), BF16)
 
         return 0
 
     lax.fori_loop(0, many, group, 0)
-    turn = regroup()
+    turn = regroup(slots)
     for part in range(STEPS // 16):
-        rows = x1[:, part * 16 : (part + 1) * 16, :].reshape(256, D)
+        rows = x1[:, part * 16 : (part + 1) * 16, :].reshape(slots * 16, D)
         turned = dot(turn, rows).astype(BF16)
         span = 16 // LOCAL
-        result[part * span : (part + 1) * span] = turned.reshape(span, LOCAL * SLOTS, D)
-
-
-def time_part(counts, tokens, gains, qkv_w, out_w):
+        result[part * span : (part + 1) * span] = turned.reshape(span, LOCAL * slots, D)
+    for fetch in fetches:
+        fetch.wait()
+
+
+def time_part(base, slots, size, arrays, later=()):
     vmem = pl.BlockSpec(memory_space=pltpu.VMEM)
     hbm = pl.BlockSpec(memory_space=pltpu.HBM)
-    return pl.pallas_call(
-        time_kernel,
-        in_specs=[pl.BlockSpec(memory_space=pltpu.SMEM), hbm, vmem, hbm, hbm],
-        out_specs=vmem,
-        out_shape=jax.ShapeDtypeStruct((GROUPS, LOCAL * SLOTS, D), BF16),
+    extra = len(later)
+    shapes = [jax.ShapeDtypeStruct((GROUPS, LOCAL * slots, D), BF16)]
+    result, *fetched = pl.pallas_call(
+        functools.partial(time_kernel, base, size, extra),
+        in_specs=[pl.BlockSpec(memory_space=pltpu.SMEM), hbm, vmem, hbm, hbm] + [hbm] * extra,
+        out_specs=[vmem] * (1 + extra),
+        out_shape=shapes + [jax.ShapeDtypeStruct(x.shape, x.dtype) for x in later],
         scratch_shapes=[
-            pltpu.VMEM((SLOTS, STEPS, D), BF16),
+            pltpu.VMEM((slots, STEPS, D), BF16),
             pltpu.VMEM((D, 3 * D), BF16),
             pltpu.VMEM((D, D), BF16),
-            pltpu.VMEM((SLOTS, STEPS, D), BF16),
-            pltpu.VMEM((ROWS, D), BF16),
-            pltpu.SemaphoreType.DMA((SLOTS // GROUP + 2 * CUTS,)),
+            pltpu.VMEM((slots, STEPS, D), BF16),
+            pltpu.VMEM((size * STEPS, D), BF16),
+            pltpu.SemaphoreType.DMA((slots // size + 2 * CUTS,)),
+            pltpu.SemaphoreType.DMA((max(extra, 1),)),
         ],
         compiler_params=pltpu.CompilerParams(vmem_limit_bytes=32 << 20),
         cost_estimate=pl.CostEstimate(
-            flops=6 << 30, bytes_accessed=4 << 20, transcendentals=1 << 20
+            flops=slots * (6 << 26), bytes_accessed=4 << 20, transcendentals=slots << 16
         ),
-        name="time_part",
-    )(counts, tokens, gains, qkv_w, out_w)
-
-
-def scene_kernel(
-    counts, recv, gains, qkv_w, out_w, in_w, back_w, result, xs, packed, ctx
-):
-    slot = iota((8, AGENTS), 1)
-    inside = slot & 15
-    place = jnp.full((8, AGENTS), -1, jnp.int32)
+        name=f"time_part_{base}_{slots}",
+    )(*(pltpu.with_memory_space_constraint(x, pltpu.HBM) for x in (*arrays, *later)))
+    return result, fetched
+
+
+def scene_kernel(parts, fetch, counts, *refs):
+    many = len(parts)
+    recv, (gains, *weights, result, xs, packed, ctx) = refs[:many], refs[many:][:9]
+    copies = []
+    if fetch:
+        *targets, sems = refs[many + 9 :]
+        sources, weights = weights[-fetch:], weights[:-fetch] + targets
+        copies = [
+            pltpu.make_async_copy(source, target, sems.at[i])
+            for i, (source, target) in enumerate(zip(sources, targets))
+        ]
+    for copy in copies:
+        copy.start()
+    qkv_w, out_w, in_w, back_w = weights
     offsets, offset = [], jnp.int32(0)
     for block in range(GROUPS):
-        count = counts[block]
-        here = ((slot >> 4) == block) & (inside < count)
-        place = jnp.where(here, inside + offset, place)
-        offsets.append((offset, count))
-        offset = offset + count
-    gather = jnp.where(iota((LIVE, AGENTS), 0) == place[0:1], 1.0, 0.0).astype(BF16)
-    for local in range(LOCAL):
-        x = recv[:, local * SLOTS : (local + 1) * SLOTS, :].reshape(AGENTS, D)
-        xs[local * LIVE : (local + 1) * LIVE] = dot(gather, x).astype(BF16)
+        offsets.append((offset, counts[block]))
+        offset = offset + counts[block]
+
+    def places(block_of, slot):
+        start, count = jnp.zeros_like(block_of), jnp.zeros_like(block_of)
+        for block, (first, live) in enumerate(offsets):
+            mine = block_of == block
+            start = jnp.where(mine, first, start)
+            count = jnp.where(mine, live, count)
+        return jnp.where(slot < count, slot + start, -1)
+
+    def gather(place):
+        return jnp.where(iota((LIVE, place.shape[1]), 0) == place[0:1], 1.0, 0.0).astype(BF16)
+
+    if many == 1:
+        column = iota((8, AGENTS), 1)
+        whole = gather(places(column >> 4, column & 15))
+        for local in range(LOCAL):
+            x = recv[0][:, local * SLOTS : (local + 1) * SLOTS, :].reshape(AGENTS, D)
+            xs[local * LIVE : (local + 1) * LIVE] = dot(whole, x).astype(BF16)
+    else:
+        placed = []
+        for base, slots in parts:
+            width = LOCAL * slots
+            column = iota((8, GROUPS * width), 1)
+            block_of = (column * (65536 // width + 1)) >> 16
+            row = column - block_of * width
+            local_of = jnp.where(row < slots, 0, 1)
+            place = places(block_of, base + row - local_of * slots)
+            placed.append((place, local_of))
+        for local in range(LOCAL):
+            x = 0.0
+            for ref, (place, local_of) in zip(recv, placed):
+                pick = gather(jnp.where(local_of == local, place, -1))
+                x = x + dot(pick, ref[...].reshape(pick.shape[1], D))
+            xs[local * LIVE : (local + 1) * LIVE] = x.astype(BF16)
 
     blocks = [slice(i * LIVE, (i + 1) * LIVE) for i in range(LOCAL)]
     for rows in blocks:
@@ -209,6 +262,8 @@
             v = packed[rows, 2 * D + low : 2 * D + low + QUAD]
             ctx[rows, low : low + QUAD] = scene_quad(q, k, v)
 
+    for copy in copies:
+        copy.wait()
     lane = iota((SLOTS, LIVE), 1) - iota((SLOTS, LIVE), 0)
     row = iota((SLOTS, LIVE), 0)
     scatter = jnp.concatenate(
@@ -227,28 +282,37 @@
         result[:, i * SLOTS : (i + 1) * SLOTS, :] = spread.reshape(GROUPS, SLOTS, D)
 
 
-def scene_part(counts, recv, gains, qkv_w, out_w, mlp_in, mlp_out):
+def scene_part(parts, recv, counts, gains, weights, fetch):
     vmem = pl.BlockSpec(memory_space=pltpu.VMEM)
+    hbm = pl.BlockSpec(memory_space=pltpu.HBM)
+    scratch = [
+        pltpu.VMEM((LOCAL * LIVE, D), BF16),
+        pltpu.VMEM((LOCAL * LIVE, 3 * D), BF16),
+        pltpu.VMEM((LOCAL * LIVE, D), BF16),
+    ]
+    weights, later = list(weights[: 4 - fetch]), weights[4 - fetch :]
+    for x in later:
+        weights.append(pltpu.with_memory_space_constraint(x, pltpu.HBM))
+        scratch.append(pltpu.VMEM(x.shape, x.dtype))
+    if fetch:
+        scratch.append(pltpu.SemaphoreType.DMA((fetch,)))
+    specs = [pl.BlockSpec(memory_space=pltpu.SMEM)] + [vmem] * (len(recv) + 5 - fetch)
     return pl.pallas_call(
-        scene_kernel,
-        in_specs=[pl.BlockSpec(memory_space=pltpu.SMEM)] + [vmem] * 6,
+        functools.partial(scene_kernel, parts, fetch),
+        in_specs=specs + [hbm] * fetch,
         out_specs=vmem,
         out_shape=jax.ShapeDtypeStruct((GROUPS, LOCAL * SLOTS, D), BF16),
-        scratch_shapes=[
-            pltpu.VMEM((LOCAL * LIVE, D), BF16),
-            pltpu.VMEM((LOCAL * LIVE, 3 * D), BF16),
-            pltpu.VMEM((LOCAL * LIVE, D), BF16),
-        ],
+        scratch_shapes=scratch,
         compiler_params=pltpu.CompilerParams(vmem_limit_bytes=40 << 20),
         cost_estimate=pl.CostEstimate(
             flops=10 << 30, bytes_accessed=8 << 20, transcendentals=2 << 20
         ),
-        name="scene_part",
-    )(counts, recv, gains, qkv_w, out_w, mlp_in, mlp_out)
+        name=f"scene_part_{len(parts)}",
+    )(counts, *recv, gains, *weights)
 
 
 def order_kernel(recv, result, turned, sems):
-    turn = regroup()
+    turn = regroup(SLOTS)
     span = 16 // LOCAL
     copies = []
     for part in range(STEPS // 16):
@@ -283,12 +347,32 @@
     return lax.all_to_all(values, "seq", split_axis=0, concat_axis=0, tiled=True)
 
 
+def one_exchange(counts, tokens, gains, qkv_time, out_time, *weights):
+    arrays = (counts, tokens, gains, qkv_time, out_time)
+    after_time, fetched = time_part(0, SLOTS, 8, arrays, weights)
+    recv = [exchange(after_time)]
+    return exchange(scene_part([(0, SLOTS)], recv, counts, gains, fetched, 0))
+
+
+def two_exchanges(counts, tokens, gains, qkv_time, out_time, *weights):
+    arrays = (counts, tokens, gains, qkv_time, out_time)
+    parts = [(0, EARLY), (EARLY, SLOTS - EARLY)]
+    early, _ = time_part(*parts[0], EARLY, arrays)
+    late, fetched = time_part(*parts[1], LATE_SIZE, arrays, weights[:2])
+    recv = [exchange(early), exchange(late)]
+    return exchange(scene_part(parts, recv, counts, gains, (*fetched, *weights[2:]), 2))
+
+
 def per_device(
     tokens, block_counts, gains, qkv_time, out_time, qkv_scene, out_scene, mlp_in, mlp_out
 ):
-    after_time = exchange(time_part(block_counts, tokens, gains, qkv_time, out_time))
-    encoded = scene_part(block_counts, after_time, gains, qkv_scene, out_scene, mlp_in, mlp_out)
-    return order_part(exchange(encoded))
+    returned = lax.cond(
+        lax.axis_index("scene") % 2 == 0,
+        one_exchange,
+        two_exchanges,
+        block_counts, tokens, gains, qkv_time, out_time, qkv_scene, out_scene, mlp_in, mlp_out,
+    )
+    return order_part(returned)
 
 
 def solution(mesh):

time: 97 us -> 85.5 us (0.88)
  the two profiles are of different devices: /device:TPU:6 before, /device:TPU:1 now
where the time goes in v4:
time: 85.5 us; the launch traced here: 84.5 us
  blocking collectives  46.7 us (55%)
  Pallas kernels  20.6 us (24%)
  starting transfers between devices  12 us (14%)
  waiting for transfers between devices  4.92 us (6%)
    all_to_all x2, blocking collectives, exchange(): lax.all_to_all(values, 'seq', split_axis=0, concat_axis=0, tiled=True)  46.7 us
    all_to_all x1, starting transfers between devices, exchange(): lax.all_to_all(values, 'seq', split_axis=0, concat_axis=0, tiled=True)  12 us
    pallas_call x2, Pallas kernels, time_part(): pl.pallas_call(functools.partial(time_kernel, base, size, extra), in_spec...  9.78 us
    pallas_call x1, Pallas kernels, scene_part(): pl.pallas_call(functools.partial(scene_kernel, parts, fetch), in_specs=sp...  9.56 us
    all_to_all x1, waiting for transfers between devices, exchange(): lax.all_to_all(values, 'seq', split_axis=0, concat_axis=0, tiled=True)  4.92 us
  transfers between devices with their start and end apart: 1, of which 1 were waited for; matrix products, arithmetic and copies ran while one was open for 0% of the time, Pallas kernels for 6%

profile of v4, /device:TPU:1, one launch (start us, length us, event | category | flops | bytes accessed | tf_op | source)
XLA Modules:
  0.0 84.5 jit_solution(12881532251599357943)
XLA Ops:
  0.0 83.1 %conditional.1 = (bf16[32,32,512]{2,1,0:T(8,128)(2,1)S(1)}) conditional(s32[]{:T(128)} %convert_element_type.3, (s32[32]{0:T(128)}, bf16[16,64,512]{2,1,0:T(8,128)(2,1)}, f32[3,512]{1,0:T(4,128)}, bf16[512,1536]{1,0:T(8,128)(2,1)}, bf16[512,512]{1,0:T(8,128)(2,1)}, /*index=5*/bf16[512,1536]{1,0:T(8,128)(2,1)}, bf16[512,512]{1,0:T(8,128)(2,1)}, ...), branch_computations={%region_0.1_spmd, %region_1.2_spmd} | conditional | flops 17179869184 | bytes 21258848 | solution.py:369
  0.0 5.1 %time_part_0_4.1 = bf16[32,8,512]{2,1,0:T(8,128)(2,1)} custom-call(s32[32]{0:T(128)} %get-tuple-element.44.counts, bf16[16,64,512]{2,1,0:T(8,128)(2,1)} %get-tuple-element.45.tokens_hbm, f32[3,512]{1,0:T(4,128)} %get-tuple-element.46.gains.refs_2_, bf16[512,1536]{1,0:T(8,128)(2,1)} %get-tuple-element.47.qkv_hbm, bf16[512,512]{1,0:T(8,128)(2,1)} %get-tuple-element.48.out_hbm), custom_call_target="tpu_custom_call" | custom-call | flops 1610612736 | bytes 4194304 | tf_op jit(solution)/shard_map/cond/branch_0_fun/time_part_0_4/pallas_call | solution.py:179
  5.1 12.0 %all-to-all-start = ((bf16[32,8,512]{2,1,0:T(8,128)(2,1)}), bf16[32,8,512]{2,1,0:T(8,128)(2,1)S(1)}, u32[]{:S(2)}, u32[]{:S(2)}) async-start(bf16[32,8,512]{2,1,0:T(8,128)(2,1)} %time_part_0_4.1), calls=%async_computation | async-start | bytes 524288 | tf_op jit(solution)/shard_map/cond/branch_0_fun/all_to_all | solution.py:347
  17.1 0.0 copy-start
  17.1 0.0 copy-start.2
  17.1 4.7 %time_part_4_12.1 = (bf16[32,24,512]{2,1,0:T(8,128)(2,1)S(1)}, bf16[512,1536]{1,0:T(8,128)(2,1)S(1)}, bf16[512,512]{1,0:T(8,128)(2,1)S(1)}) custom-call(s32[32]{0:T(128)} %get-tuple-element.44.counts, bf16[16,64,512]{2,1,0:T(8,128)(2,1)} %get-tuple-element.45.tokens_hbm, f32[3,512]{1,0:T(4,128)} %get-tuple-element.46.gains.refs_2_, ...), custom_call_target="tpu_custom_call" | custom-call | flops 4831838208 | bytes 4194304 | tf_op jit(solution)/shard_map/cond/branch_0_fun/time_part_4_12/pallas_call | solution.py:179
  21.9 4.9 %all-to-all-done.refs_0_ = bf16[32,8,512]{2,1,0:T(8,128)(2,1)S(1)} async-done(((bf16[32,8,512]{2,1,0:T(8,128)(2,1)}), bf16[32,8,512]{2,1,0:T(8,128)(2,1)S(1)}, u32[]{:S(2)}, u32[]{:S(2)}) %all-to-all-start) | async-done | bytes 262176 | tf_op jit(solution)/shard_map/cond/branch_0_fun/all_to_all | solution.py:347
  26.8 21.9 %all_to_all.20.refs_1_ = bf16[32,24,512]{2,1,0:T(8,128)(2,1)S(1)} all-to-all(bf16[32,24,512]{2,1,0:T(8,128)(2,1)S(1)} %get-tuple-element.51), channel_id=1, replica_groups=mesh['scene'=8,'seq'=32] {'seq'}, dimensions={0} | all-to-all | bytes 1572864 | tf_op jit(solution)/shard_map/cond/branch_0_fun/all_to_all | solution.py:347
  48.6 0.0 copy-done
  48.6 0.0 copy-done.2
  48.6 9.6 %scene_part_2.1 = bf16[32,32,512]{2,1,0:T(8,128)(2,1)S(1)} custom-call(s32[32]{0:T(128)S(1)} %copy-done.2, bf16[32,8,512]{2,1,0:T(8,128)(2,1)S(1)} %all-to-all-done.refs_0_, bf16[32,24,512]{2,1,0:T(8,128)(2,1)S(1)} %all_to_all.20.refs_1_, f32[3,512]{1,0:T(4,128)S(1)} %copy-done, bf16[512,1536]{1,0:T(8,128)(2,1)S(1)} %get-tuple-element.52.refs_3_, ...), custom_call_target="tpu_custom_call" | custom-call | flops 10737418240 | bytes 8388608 | tf_op jit(solution)/shard_map/cond/branch_0_fun/scene_part_2/pallas_call | solution.py:300
  58.2 24.9 %all_to_all.21 = bf16[32,32,512]{2,1,0:T(8,128)(2,1)S(1)} all-to-all(bf16[32,32,512]{2,1,0:T(8,128)(2,1)S(1)} %scene_part_2.1), channel_id=1, replica_groups=mesh['scene'=8,'seq'=32] {'seq'}, dimensions={0} | all-to-all | bytes 2097152 | tf_op jit(solution)/shard_map/cond/branch_0_fun/all_to_all | solution.py:347
  83.1 1.2 %order_part.1 = bf16[16,64,512]{2,1,0:T(8,128)(2,1)} custom-call(bf16[32,32,512]{2,1,0:T(8,128)(2,1)S(1)} %get-tuple-element.70.recv), custom_call_target="tpu_custom_call" | custom-call | tf_op jit(solution)/shard_map/order_part/pallas_call | solution.py:332
Async XLA Ops:
  5.1 21.7 %all-to-all-start = ((bf16[32,8,512]{2,1,0:T(8,128)(2,1)}), bf16[32,8,512]{2,1,0:T(8,128)(2,1)S(1)}, u32[]{:S(2)}, u32[]{:S(2)}) async-start(bf16[32,8,512]{2,1,0:T(8,128)(2,1)} %time_part_0_4.1), calls=%async_computation | async-start | bytes 524288 | tf_op jit(solution)/shard_map/cond/branch_0_fun/all_to_all | solution.py:347
  17.1 31.5 %copy-start = (f32[3,512]{1,0:T(4,128)S(1)}, f32[3,512]{1,0:T(4,128)}, u32[]{:S(2)}) copy-start(f32[3,512]{1,0:T(4,128)} %get-tuple-element.46.gains.refs_2_) | copy-start | bytes 18436 | tf_op jit(solution)/shard_map/cond
  17.1 31.5 %copy-start.2 = (s32[32]{0:T(128)S(1)}, s32[32]{0:T(128)}, u32[]{:S(2)}) copy-start(s32[32]{0:T(128)} %get-tuple-element.44.counts) | copy-start | bytes 388 | tf_op jit(solution)/shard_map/cond

commit v5 on v4

--- a/solution.py
+++ b/solution.py
@@ -21,6 +21,7 @@
 INV_ROOT = 0.125
 EARLY = 4
 LATE_SIZE = 4
+KEEP = False
 CUTS = 4
 BF16 = jnp.bfloat16
 F32 = jnp.float32
@@ -55,9 +56,9 @@
     return jnp.concatenate([jnp.where(lane == h, k, jnp.zeros_like(k)) for h in range(4)], axis=0)
 
 
-def time_group(values, gains, qkv_w, out_w, ctx):
+def time_group(values, normed, qkv_w, out_w, ctx):
     agents = values.shape[0] // STEPS
-    packed = dot(rms(values, gains[0:1, :]), qkv_w[...]).astype(BF16)
+    packed = dot(normed, qkv_w[...]).astype(BF16)
     ones = quad_masks(jnp.ones((STEPS, QUAD), BF16))
     for agent in range(agents):
         rows = slice(agent * STEPS, (agent + 1) * STEPS)
@@ -104,54 +105,60 @@
     return (value * jnp.concatenate(inverse, axis=1)).astype(BF16)
 
 
-def time_kernel(base, size, extra, counts, tokens_hbm, gains, qkv_hbm, out_hbm, *refs):
-    later_hbm, (result, *later) = refs[:extra], refs[extra : 2 * extra + 1]
-    tokens, qkv_w, out_w, x1, ctx, sems, later_sems = refs[2 * extra + 1 :]
+def time_kernel(base, size, own, keep, extra, counts_hbm, tokens_hbm, gains_hbm, *refs):
+    refs = list(refs)
+    take = lambda many: [refs.pop(0) for _ in range(many)]
+    sources, later_hbm, (result,) = take(2), take(extra), take(1)
+    kept, later, (counts, gains, tokens) = take(2 * keep), take(extra), take(3)
+    weights = (kept or take(2)) if own else sources
+    x1, ctx, sems, token_sems, weight_sems, later_sems = refs
     slots = tokens.shape[0]
     many = slots // size
     cut = D // CUTS
+    small = [
+        pltpu.make_async_copy(counts_hbm, counts, sems.at[0]),
+        pltpu.make_async_copy(gains_hbm, gains, sems.at[1]),
+    ]
 
     def tokens_copy(i):
         first = pl.multiple_of(i * size, size)
         source = tokens_hbm.at[pl.ds(base + first, size)]
-        return pltpu.make_async_copy(source, tokens.at[pl.ds(first, size)], sems.at[i])
-
-    def weight_copies(source, target, first):
-        parts = [pl.ds(i * cut, cut) for i in range(CUTS)]
-        return [
-            pltpu.make_async_copy(source.at[part], target.at[part], sems.at[first + i])
-            for i, part in enumerate(parts)
-        ]
-
+        return pltpu.make_async_copy(source, tokens.at[pl.ds(first, size)], token_sems.at[i])
+
+    weight_copies = [
+        pltpu.make_async_copy(
+            sources[w].at[pl.ds(i * cut, cut)],
+            weights[w].at[pl.ds(i * cut, cut)],
+            weight_sems.at[w * CUTS + i],
+        )
+        for w in range(2 * own)
+        for i in range(CUTS)
+    ]
     tokens_copy(0).start()
-    weights = weight_copies(qkv_hbm, qkv_w, many) + weight_copies(out_hbm, out_w, many + CUTS)
-    for copy in weights:
+    for copy in small + weight_copies:
         copy.start()
     for i in range(1, many):
         tokens_copy(i).start()
+    for copy in small:
+        copy.wait()
     count = counts[lax.axis_index("seq")]
-    for copy in weights[:CUTS]:
-        copy.wait()
-    fetches = [
-        pltpu.make_async_copy(source, target, later_sems.at[i])
-        for i, (source, target) in enumerate(zip(later_hbm, later))
-    ]
-    for fetch in fetches:
-        fetch.start()
 
     def group(i, _):
         first = pl.multiple_of(i * size, size)
         tokens_copy(i).wait()
+        values = tokens[pl.ds(first, size)].reshape(size * STEPS, D)
+        normed = rms(values, gains[0:1, :])
 
         @pl.when(i == 0)
         def _():
-            for copy in weights[CUTS:]:
+            for copy in weight_copies:
                 copy.wait()
+            for source, target, sem in zip(later_hbm, later, range(extra)):
+                pltpu.make_async_copy(source, target, later_sems.at[sem]).start()
 
         @pl.when(base + first < count)
         def _():
-            values = tokens[pl.ds(first, size)].reshape(size * STEPS, D)
-            after = time_group(values, gains, qkv_w, out_w, ctx)
+            after = time_group(values, normed, *weights, ctx)
             x1[pl.ds(first, size)] = after.reshape(size, STEPS, D)
 
         @pl.when(base + first >= count)
@@ -167,27 +174,34 @@
         turned = dot(turn, rows).astype(BF16)
         span = 16 // LOCAL
         result[part * span : (part + 1) * span] = turned.reshape(span, LOCAL * slots, D)
-    for fetch in fetches:
-        fetch.wait()
-
-
-def time_part(base, slots, size, arrays, later=()):
+    for source, target, sem in zip(later_hbm, later, range(extra)):
+        pltpu.make_async_copy(source, target, later_sems.at[sem]).wait()
+
+
+def time_part(base, slots, size, arrays, weights, own=True, keep=False, later=()):
     vmem = pl.BlockSpec(memory_space=pltpu.VMEM)
     hbm = pl.BlockSpec(memory_space=pltpu.HBM)
     extra = len(later)
-    shapes = [jax.ShapeDtypeStruct((GROUPS, LOCAL * slots, D), BF16)]
-    result, *fetched = pl.pallas_call(
-        functools.partial(time_kernel, base, size, extra),
-        in_specs=[pl.BlockSpec(memory_space=pltpu.SMEM), hbm, vmem, hbm, hbm] + [hbm] * extra,
-        out_specs=[vmem] * (1 + extra),
-        out_shape=shapes + [jax.ShapeDtypeStruct(x.shape, x.dtype) for x in later],
+    pin = lambda xs: [pltpu.with_memory_space_constraint(x, pltpu.HBM) for x in xs]
+    like = lambda xs: [jax.ShapeDtypeStruct(x.shape, x.dtype) for x in xs]
+    given = [] if keep or not own else [pltpu.VMEM(x.shape, x.dtype) for x in weights]
+    result, *others = pl.pallas_call(
+        functools.partial(time_kernel, base, size, own, keep, extra),
+        in_specs=[hbm] * 3 + [hbm if own else vmem] * 2 + [hbm] * extra,
+        out_specs=[vmem] * (1 + 2 * keep + extra),
+        out_shape=[jax.ShapeDtypeStruct((GROUPS, LOCAL * slots, D), BF16)]
+        + (like(weights) if keep else [])
+        + like(later),
         scratch_shapes=[
+            pltpu.SMEM((GROUPS,), jnp.int32),
+            pltpu.VMEM((3, D), F32),
             pltpu.VMEM((slots, STEPS, D), BF16),
-            pltpu.VMEM((D, 3 * D), BF16),
-            pltpu.VMEM((D, D), BF16),
+            *given,
             pltpu.VMEM((slots, STEPS, D), BF16),
             pltpu.VMEM((size * STEPS, D), BF16),
-            pltpu.SemaphoreType.DMA((slots // size + 2 * CUTS,)),
+            pltpu.SemaphoreType.DMA((2,)),
+            pltpu.SemaphoreType.DMA((slots // size,)),
+            pltpu.SemaphoreType.DMA((2 * CUTS,)),
             pltpu.SemaphoreType.DMA((max(extra, 1),)),
         ],
         compiler_params=pltpu.CompilerParams(vmem_limit_bytes=32 << 20),
@@ -195,16 +209,22 @@
             flops=slots * (6 << 26), bytes_accessed=4 << 20, transcendentals=slots << 16
         ),
         name=f"time_part_{base}_{slots}",
-    )(*(pltpu.with_memory_space_constraint(x, pltpu.HBM) for x in (*arrays, *later)))
-    return result, fetched
-
-
-def scene_kernel(parts, fetch, counts, *refs):
-    many = len(parts)
-    recv, (gains, *weights, result, xs, packed, ctx) = refs[:many], refs[many:][:9]
+    )(*pin(arrays), *(pin(weights) if own else weights), *pin(later))
+    return result, others
+
+
+def mlp_rows(x1, o2, gains, in_w, back_w):
+    x2 = (x1.astype(F32) + o2.astype(F32)).astype(BF16)
+    hidden = jnp.maximum(dot(rms(x2, gains[2:3, :]), in_w[...]), 0.0).astype(BF16)
+    return (x2.astype(F32) + dot(hidden, back_w[...])).astype(BF16)
+
+
+def scene_kernel(parts, mlp, fetch, counts, *refs):
+    many, end = len(parts), len(parts) + 7 + 2 * mlp
+    recv, (gains, *weights, result, xs, packed, ctx) = refs[:many], refs[many:end]
     copies = []
     if fetch:
-        *targets, sems = refs[many + 9 :]
+        *targets, sems = refs[end:]
         sources, weights = weights[-fetch:], weights[:-fetch] + targets
         copies = [
             pltpu.make_async_copy(source, target, sems.at[i])
@@ -212,7 +232,7 @@
         ]
     for copy in copies:
         copy.start()
-    qkv_w, out_w, in_w, back_w = weights
+    qkv_w, out_w = weights[:2]
     offsets, offset = [], jnp.int32(0)
     for block in range(GROUPS):
         offsets.append((offset, counts[block]))
@@ -275,9 +295,7 @@
     )
     for i, rows in enumerate(blocks):
         o2 = dot(ctx[rows], out_w[...]).astype(BF16)
-        x2 = (xs[rows].astype(F32) + o2.astype(F32)).astype(BF16)
-        hidden = jnp.maximum(dot(rms(x2, gains[2:3, :]), in_w[...]), 0.0).astype(BF16)
-        encoded = (x2.astype(F32) + dot(hidden, back_w[...])).astype(BF16)
+        encoded = mlp_rows(xs[rows], o2, gains, *weights[2:]) if mlp else o2
         spread = dot(scatter, encoded).astype(BF16)
         result[:, i * SLOTS : (i + 1) * SLOTS, :] = spread.reshape(GROUPS, SLOTS, D)
 
@@ -290,15 +308,16 @@
         pltpu.VMEM((LOCAL * LIVE, 3 * D), BF16),
         pltpu.VMEM((LOCAL * LIVE, D), BF16),
     ]
-    weights, later = list(weights[: 4 - fetch]), weights[4 - fetch :]
+    mlp, now = len(weights) == 4, len(weights) - fetch
+    weights, later = list(weights[:now]), weights[now:]
     for x in later:
         weights.append(pltpu.with_memory_space_constraint(x, pltpu.HBM))
         scratch.append(pltpu.VMEM(x.shape, x.dtype))
     if fetch:
         scratch.append(pltpu.SemaphoreType.DMA((fetch,)))
-    specs = [pl.BlockSpec(memory_space=pltpu.SMEM)] + [vmem] * (len(recv) + 5 - fetch)
+    specs = [pl.BlockSpec(memory_space=pltpu.SMEM)] + [vmem] * (len(recv) + 1 + now)
     return pl.pallas_call(
-        functools.partial(scene_kernel, parts, fetch),
+        functools.partial(scene_kernel, parts, mlp, fetch),
         in_specs=specs + [hbm] * fetch,
         out_specs=vmem,
         out_shape=jax.ShapeDtypeStruct((GROUPS, LOCAL * SLOTS, D), BF16),
@@ -309,6 +328,35 @@
         ),
         name=f"scene_part_{len(parts)}",
     )(counts, *recv, gains, *weights)
+
+
+def mlp_kernel(counts, x1, o2, gains, in_w, back_w, result):
+    count = counts[lax.axis_index("seq")]
+    span = 16 // LOCAL
+
+    def part(i, _):
+        here = pl.ds(pl.multiple_of(i * span, span), span)
+        rows = (span * LOCAL * SLOTS, D)
+        encoded = mlp_rows(x1[here].reshape(rows), o2[here].reshape(rows), gains, in_w, back_w)
+        live = (iota(rows, 0) & (SLOTS - 1)) < count
+        encoded = jnp.where(live, encoded.astype(F32), 0.0).astype(BF16)
+        result[here] = encoded.reshape(span, LOCAL * SLOTS, D)
+        return 0
+
+    lax.fori_loop(0, GROUPS // span, part, 0)
+
+
+def mlp_part(counts, x1, o2, gains, in_w, back_w):
+    vmem = pl.BlockSpec(memory_space=pltpu.VMEM)
+    return pl.pallas_call(
+        mlp_kernel,
+        in_specs=[pl.BlockSpec(memory_space=pltpu.SMEM)] + [vmem] * 5,
+        out_specs=vmem,
+        out_shape=jax.ShapeDtypeStruct((GROUPS, LOCAL * SLOTS, D), BF16),
+        compiler_params=pltpu.CompilerParams(vmem_limit_bytes=24 << 20),
+        cost_estimate=pl.CostEstimate(flops=4 << 30, bytes_accessed=6 << 20, transcendentals=0),
+        name="mlp_part",
+    )(counts, x1, o2, gains, in_w, back_w)
 
 
 def order_kernel(recv, result, turned, sems):
@@ -347,20 +395,23 @@
     return lax.all_to_all(values, "seq", split_axis=0, concat_axis=0, tiled=True)
 
 
-def one_exchange(counts, tokens, gains, qkv_time, out_time, *weights):
-    arrays = (counts, tokens, gains, qkv_time, out_time)
-    after_time, fetched = time_part(0, SLOTS, 8, arrays, weights)
+def one_exchange(counts, tokens, gains, qkv_time, out_time, *later):
+    arrays, weights = (counts, tokens, gains), (qkv_time, out_time)
+    after_time, fetched = time_part(0, SLOTS, 8, arrays, weights, later=later[:2])
     recv = [exchange(after_time)]
-    return exchange(scene_part([(0, SLOTS)], recv, counts, gains, fetched, 0))
-
-
-def two_exchanges(counts, tokens, gains, qkv_time, out_time, *weights):
-    arrays = (counts, tokens, gains, qkv_time, out_time)
+    o2 = exchange(scene_part([(0, SLOTS)], recv, counts, gains, fetched, 0))
+    return mlp_part(counts, after_time, o2, gains, *later[2:])
+
+
+def two_exchanges(counts, tokens, gains, qkv_time, out_time, *later):
+    arrays, weights = (counts, tokens, gains), (qkv_time, out_time)
     parts = [(0, EARLY), (EARLY, SLOTS - EARLY)]
-    early, _ = time_part(*parts[0], EARLY, arrays)
-    late, fetched = time_part(*parts[1], LATE_SIZE, arrays, weights[:2])
+    early, kept = time_part(*parts[0], EARLY, arrays, weights, keep=KEEP)
+    late, fetched = time_part(
+        *parts[1], LATE_SIZE, arrays, kept or weights, own=not KEEP, later=later[:2]
+    )
     recv = [exchange(early), exchange(late)]
-    return exchange(scene_part(parts, recv, counts, gains, (*fetched, *weights[2:]), 2))
+    return exchange(scene_part(parts, recv, counts, gains, (*fetched, *later[2:]), 2))
 
 
 def per_device(

time: 85.5 us -> 81.2 us (0.950)
  blocking collectives: 46.7 us -> 43.6 us
  waiting for transfers between devices: 4.92 us -> 1.93 us
  Pallas kernels: 20.6 us -> 22.9 us
    all_to_all x2, blocking collectives: 46.7 us -> 43.6 us  [exchange(): lax.all_to_all(values, 'seq', split_axis=0, concat_axis=0, tiled=True)]
    all_to_all x1, waiting for transfers between devices: 4.92 us -> 1.93 us  [exchange(): lax.all_to_all(values, 'seq', split_axis=0, concat_axis=0, tiled=True)]
    pallas_call x3, Pallas kernels: 19.3 us -> 21.7 us  [the longest x2 12.1 us: time_part(): pl.pallas_call(functools.partial(time_kernel, base, size, own, keep, extr...]
  transfers between devices with their start and end apart: 1 -> 1, of which waited for: 1 -> 1; matrix products, arithmetic and copies ran while one was open for 0% -> 0% of each run, Pallas kernels for 6% -> 10%
where the time goes in v5:
time: 81.2 us; the launch traced here: 80.8 us
  blocking collectives  43.6 us (54%)
  Pallas kernels  22.9 us (28%)
  starting transfers between devices  12 us (15%)
  waiting for transfers between devices  1.93 us (2%)
    all_to_all x2, blocking collectives, exchange(): lax.all_to_all(values, 'seq', split_axis=0, concat_axis=0, tiled=True)  43.6 us
    pallas_call x2, Pallas kernels, time_part(): pl.pallas_call(functools.partial(time_kernel, base, size, own, keep, extr...  12.1 us
    all_to_all x1, starting transfers between devices, exchange(): lax.all_to_all(values, 'seq', split_axis=0, concat_axis=0, tiled=True)  12 us
    pallas_call x1, Pallas kernels, scene_part(): pl.pallas_call(functools.partial(scene_kernel, parts, mlp, fetch), in_spe...  9.57 us
    all_to_all x1, waiting for transfers between devices, exchange(): lax.all_to_all(values, 'seq', split_axis=0, concat_axis=0, tiled=True)  1.93 us
  transfers between devices with their start and end apart: 1, of which 1 were waited for; matrix products, arithmetic and copies ran while one was open for 0% of the time, Pallas kernels for 10%

profile of v5, /device:TPU:1, one launch (start us, length us, event | category | flops | bytes accessed | tf_op | source)
XLA Modules:
  0.0 80.8 jit_solution(1622402937214365890)
XLA Ops:
  0.0 79.4 %conditional.1 = (bf16[32,32,512]{2,1,0:T(8,128)(2,1)S(1)}) conditional(s32[]{:T(128)} %convert_element_type.3, (s32[32]{0:T(128)}, bf16[16,64,512]{2,1,0:T(8,128)(2,1)}, f32[3,512]{1,0:T(4,128)}, bf16[512,1536]{1,0:T(8,128)(2,1)}, bf16[512,512]{1,0:T(8,128)(2,1)}, /*index=5*/bf16[512,1536]{1,0:T(8,128)(2,1)}, bf16[512,512]{1,0:T(8,128)(2,1)}, ...), branch_computations={%region_0.1_spmd, %region_1.2_spmd} | conditional | flops 21474836480 | bytes 39871096 | solution.py:420
  0.0 4.4 %time_part_0_4.1 = bf16[32,8,512]{2,1,0:T(8,128)(2,1)} custom-call(s32[32]{0:T(128)} %get-tuple-element.44.counts_hbm.counts, bf16[16,64,512]{2,1,0:T(8,128)(2,1)} %get-tuple-element.45.tokens_hbm, f32[3,512]{1,0:T(4,128)} %get-tuple-element.46.gains_hbm.refs_2_, bf16[512,1536]{1,0:T(8,128)(2,1)} %get-tuple-element.47.refs_0_, ...), custom_call_target="tpu_custom_call" | custom-call | flops 1610612736 | bytes 4194304 | tf_op jit(solution)/shard_map/cond/branch_0_fun/time_part_0_4/pallas_call | solution.py:188
  4.4 12.0 %all-to-all-start = ((bf16[32,8,512]{2,1,0:T(8,128)(2,1)}), bf16[32,8,512]{2,1,0:T(8,128)(2,1)S(1)}, u32[]{:S(2)}, u32[]{:S(2)}) async-start(bf16[32,8,512]{2,1,0:T(8,128)(2,1)} %time_part_0_4.1), calls=%async_computation | async-start | bytes 524288 | tf_op jit(solution)/shard_map/cond/branch_0_fun/all_to_all | solution.py:395
  16.5 7.7 %time_part_4_12.1 = (bf16[32,24,512]{2,1,0:T(8,128)(2,1)S(1)}, bf16[512,1536]{1,0:T(8,128)(2,1)S(1)}, bf16[512,512]{1,0:T(8,128)(2,1)S(1)}) custom-call(s32[32]{0:T(128)} %get-tuple-element.44.counts_hbm.counts, bf16[16,64,512]{2,1,0:T(8,128)(2,1)} %get-tuple-element.45.tokens_hbm, f32[3,512]{1,0:T(4,128)} %get-tuple-element.46.gains_hbm.refs_2_, ...), custom_call_target="tpu_custom_call" | custom-call | flops 4831838208 | bytes 4194304 | tf_op jit(solution)/shard_map/cond/branch_0_fun/time_part_4_12/pallas_call | solution.py:188
  24.2 0.0 copy-start.2
  24.2 0.0 copy-start.4
  24.2 1.9 %all-to-all-done.refs_0_ = bf16[32,8,512]{2,1,0:T(8,128)(2,1)S(1)} async-done(((bf16[32,8,512]{2,1,0:T(8,128)(2,1)}), bf16[32,8,512]{2,1,0:T(8,128)(2,1)S(1)}, u32[]{:S(2)}, u32[]{:S(2)}) %all-to-all-start) | async-done | bytes 262176 | tf_op jit(solution)/shard_map/cond/branch_0_fun/all_to_all | solution.py:395
  26.1 21.3 %all_to_all.20.refs_1_ = bf16[32,24,512]{2,1,0:T(8,128)(2,1)S(1)} all-to-all(bf16[32,24,512]{2,1,0:T(8,128)(2,1)S(1)} %get-tuple-element.51), channel_id=1, replica_groups=mesh['scene'=8,'seq'=32] {'seq'}, dimensions={0} | all-to-all | bytes 1572864 | tf_op jit(solution)/shard_map/cond/branch_0_fun/all_to_all | solution.py:395
  47.5 0.0 copy-done.2
  47.5 0.0 copy-done.4
  47.5 9.6 %scene_part_2.1 = bf16[32,32,512]{2,1,0:T(8,128)(2,1)S(1)} custom-call(s32[32]{0:T(128)S(1)} %copy-done.4, bf16[32,8,512]{2,1,0:T(8,128)(2,1)S(1)} %all-to-all-done.refs_0_, bf16[32,24,512]{2,1,0:T(8,128)(2,1)S(1)} %all_to_all.20.refs_1_, f32[3,512]{1,0:T(4,128)S(1)} %copy-done.2, bf16[512,1536]{1,0:T(8,128)(2,1)S(1)} %get-tuple-element.52.refs_3_, ...), custom_call_target="tpu_custom_call" | custom-call | flops 10737418240 | bytes 8388608 | tf_op jit(solution)/shard_map/cond/branch_0_fun/scene_part_2/pallas_call | solution.py:319
  57.0 22.3 %all_to_all.21 = bf16[32,32,512]{2,1,0:T(8,128)(2,1)S(1)} all-to-all(bf16[32,32,512]{2,1,0:T(8,128)(2,1)S(1)} %scene_part_2.1), channel_id=1, replica_groups=mesh['scene'=8,'seq'=32] {'seq'}, dimensions={0} | all-to-all | bytes 2097152 | tf_op jit(solution)/shard_map/cond/branch_0_fun/all_to_all | solution.py:395
  79.4 1.2 %order_part.1 = bf16[16,64,512]{2,1,0:T(8,128)(2,1)} custom-call(bf16[32,32,512]{2,1,0:T(8,128)(2,1)S(1)} %get-tuple-element.68.recv), custom_call_target="tpu_custom_call" | custom-call | tf_op jit(solution)/shard_map/order_part/pallas_call | solution.py:380
Async XLA Ops:
  4.4 21.7 %all-to-all-start = ((bf16[32,8,512]{2,1,0:T(8,128)(2,1)}), bf16[32,8,512]{2,1,0:T(8,128)(2,1)S(1)}, u32[]{:S(2)}, u32[]{:S(2)}) async-start(bf16[32,8,512]{2,1,0:T(8,128)(2,1)} %time_part_0_4.1), calls=%async_computation | async-start | bytes 524288 | tf_op jit(solution)/shard_map/cond/branch_0_fun/all_to_all | solution.py:395
  24.2 23.3 %copy-start.2 = (f32[3,512]{1,0:T(4,128)S(1)}, f32[3,512]{1,0:T(4,128)}, u32[]{:S(2)}) copy-start(f32[3,512]{1,0:T(4,128)} %get-tuple-element.46.gains_hbm.refs_2_) | copy-start | bytes 18436 | tf_op jit(solution)/shard_map/cond
  24.2 23.3 %copy-start.4 = (s32[32]{0:T(128)S(1)}, s32[32]{0:T(128)}, u32[]{:S(2)}) copy-start(s32[32]{0:T(128)} %get-tuple-element.44.counts_hbm.counts) | copy-start | bytes 388 | tf_op jit(solution)/shard_map/cond

commit v6 on v5

--- a/solution.py
+++ b/solution.py
@@ -20,9 +20,6 @@
 LOWEST = -3e38
 INV_ROOT = 0.125
 EARLY = 4
-LATE_SIZE = 4
-KEEP = False
-CUTS = 4
 BF16 = jnp.bfloat16
 F32 = jnp.float32
 
@@ -56,9 +53,9 @@
     return jnp.concatenate([jnp.where(lane == h, k, jnp.zeros_like(k)) for h in range(4)], axis=0)
 
 
-def time_group(values, normed, qkv_w, out_w, ctx):
+def time_group(values, normed, qkv_w, out_w, ctx, packed):
     agents = values.shape[0] // STEPS
-    packed = dot(normed, qkv_w[...]).astype(BF16)
+    packed[...] = dot(normed, qkv_w[...]).astype(BF16)
     ones = quad_masks(jnp.ones((STEPS, QUAD), BF16))
     for agent in range(agents):
         rows = slice(agent * STEPS, (agent + 1) * STEPS)
@@ -105,16 +102,14 @@
     return (value * jnp.concatenate(inverse, axis=1)).astype(BF16)
 
 
-def time_kernel(base, size, own, keep, extra, counts_hbm, tokens_hbm, gains_hbm, *refs):
+def time_kernel(base, size, extra, counts_hbm, tokens_hbm, gains_hbm, *refs):
     refs = list(refs)
     take = lambda many: [refs.pop(0) for _ in range(many)]
     sources, later_hbm, (result,) = take(2), take(extra), take(1)
-    kept, later, (counts, gains, tokens) = take(2 * keep), take(extra), take(3)
-    weights = (kept or take(2)) if own else sources
-    x1, ctx, sems, token_sems, weight_sems, later_sems = refs
+    later, (counts, gains, tokens), weights = take(extra), take(3), take(2)
+    x1, ctx, packed, sems, token_sems, weight_sems, later_sems = refs
     slots = tokens.shape[0]
     many = slots // size
-    cut = D // CUTS
     small = [
         pltpu.make_async_copy(counts_hbm, counts, sems.at[0]),
         pltpu.make_async_copy(gains_hbm, gains, sems.at[1]),
@@ -126,14 +121,9 @@
         return pltpu.make_async_copy(source, tokens.at[pl.ds(first, size)], token_sems.at[i])
 
     weight_copies = [
-        pltpu.make_async_copy(
-            sources[w].at[pl.ds(i * cut, cut)],
-            weights[w].at[pl.ds(i * cut, cut)],
-            weight_sems.at[w * CUTS + i],
-        )
-        for w in range(2 * own)
-        for i in range(CUTS)
+        pltpu.make_async_copy(sources[w], weights[w], weight_sems.at[w]) for w in range(2)
     ]
+
     tokens_copy(0).start()
     for copy in small + weight_copies:
         copy.start()
@@ -158,7 +148,7 @@
 
         @pl.when(base + first < count)
         def _():
-            after = time_group(values, normed, *weights, ctx)
+            after = time_group(values, normed, *weights, ctx, packed)
             x1[pl.ds(first, size)] = after.reshape(size, STEPS, D)
 
         @pl.when(base + first >= count)
@@ -178,30 +168,28 @@
         pltpu.make_async_copy(source, target, later_sems.at[sem]).wait()
 
 
-def time_part(base, slots, size, arrays, weights, own=True, keep=False, later=()):
+def time_part(base, slots, size, arrays, weights, later=()):
     vmem = pl.BlockSpec(memory_space=pltpu.VMEM)
     hbm = pl.BlockSpec(memory_space=pltpu.HBM)
     extra = len(later)
     pin = lambda xs: [pltpu.with_memory_space_constraint(x, pltpu.HBM) for x in xs]
-    like = lambda xs: [jax.ShapeDtypeStruct(x.shape, x.dtype) for x in xs]
-    given = [] if keep or not own else [pltpu.VMEM(x.shape, x.dtype) for x in weights]
     result, *others = pl.pallas_call(
-        functools.partial(time_kernel, base, size, own, keep, extra),
-        in_specs=[hbm] * 3 + [hbm if own else vmem] * 2 + [hbm] * extra,
-        out_specs=[vmem] * (1 + 2 * keep + extra),
+        functools.partial(time_kernel, base, size, extra),
+        in_specs=[hbm] * (5 + extra),
+        out_specs=[vmem] * (1 + extra),
         out_shape=[jax.ShapeDtypeStruct((GROUPS, LOCAL * slots, D), BF16)]
-        + (like(weights) if keep else [])
-        + like(later),
+        + [jax.ShapeDtypeStruct(x.shape, x.dtype) for x in later],
         scratch_shapes=[
             pltpu.SMEM((GROUPS,), jnp.int32),
             pltpu.VMEM((3, D), F32),
             pltpu.VMEM((slots, STEPS, D), BF16),
-            *given,
+            *(pltpu.VMEM(x.shape, x.dtype) for x in weights),
             pltpu.VMEM((slots, STEPS, D), BF16),
             pltpu.VMEM((size * STEPS, D), BF16),
+            pltpu.VMEM((size * STEPS, 3 * D), BF16),
             pltpu.SemaphoreType.DMA((2,)),
             pltpu.SemaphoreType.DMA((slots // size,)),
-            pltpu.SemaphoreType.DMA((2 * CUTS,)),
+            pltpu.SemaphoreType.DMA((2,)),
             pltpu.SemaphoreType.DMA((max(extra, 1),)),
         ],
         compiler_params=pltpu.CompilerParams(vmem_limit_bytes=32 << 20),
@@ -209,7 +197,7 @@
             flops=slots * (6 << 26), bytes_accessed=4 << 20, transcendentals=slots << 16
         ),
         name=f"time_part_{base}_{slots}",
-    )(*pin(arrays), *(pin(weights) if own else weights), *pin(later))
+    )(*pin(arrays), *pin(weights), *pin(later))
     return result, others
 
 
@@ -282,8 +270,6 @@
             v = packed[rows, 2 * D + low : 2 * D + low + QUAD]
             ctx[rows, low : low + QUAD] = scene_quad(q, k, v)
 
-    for copy in copies:
-        copy.wait()
     lane = iota((SLOTS, LIVE), 1) - iota((SLOTS, LIVE), 0)
     row = iota((SLOTS, LIVE), 0)
     scatter = jnp.concatenate(
@@ -295,6 +281,9 @@
     )
     for i, rows in enumerate(blocks):
         o2 = dot(ctx[rows], out_w[...]).astype(BF16)
+        if i == 0:
+            for copy in copies:
+                copy.wait()
         encoded = mlp_rows(xs[rows], o2, gains, *weights[2:]) if mlp else o2
         spread = dot(scatter, encoded).astype(BF16)
         result[:, i * SLOTS : (i + 1) * SLOTS, :] = spread.reshape(GROUPS, SLOTS, D)
@@ -406,9 +395,9 @@
 def two_exchanges(counts, tokens, gains, qkv_time, out_time, *later):
     arrays, weights = (counts, tokens, gains), (qkv_time, out_time)
     parts = [(0, EARLY), (EARLY, SLOTS - EARLY)]
-    early, kept = time_part(*parts[0], EARLY, arrays, weights, keep=KEEP)
+    early, _ = time_part(*parts[0], EARLY, arrays, weights)
     late, fetched = time_part(
-        *parts[1], LATE_SIZE, arrays, kept or weights, own=not KEEP, later=later[:2]
+        *parts[1], 4, arrays, weights, later=later[:2]
     )
     recv = [exchange(early), exchange(late)]
     return exchange(scene_part(parts, recv, counts, gains, (*fetched, *later[2:]), 2))

time: 81.2 us -> 82 us (level)
  blocking collectives: 43.6 us -> 44.6 us
    all_to_all x2, blocking collectives: 43.6 us -> 44.6 us  [exchange(): lax.all_to_all(values, 'seq', split_axis=0, concat_axis=0, tiled=True)]
  transfers between devices with their start and end apart: 1 -> 1, of which waited for: 1 -> 1; matrix products, arithmetic and copies ran while one was open for 0% -> 0% of each run, Pallas kernels for 10% -> 9%
where the time goes in v6:
time: 82 us; the launch traced here: 81.2 us
  blocking collectives  44.6 us (54%)
  Pallas kernels  22.3 us (27%)
  starting transfers between devices  12 us (15%)
  waiting for transfers between devices  2.04 us (2%)
    all_to_all x2, blocking collectives, exchange(): lax.all_to_all(values, 'seq', split_axis=0, concat_axis=0, tiled=True)  44.6 us
    all_to_all x1, starting transfers between devices, exchange(): lax.all_to_all(values, 'seq', split_axis=0, concat_axis=0, tiled=True)  12 us
    pallas_call x2, Pallas kernels, time_part(): pl.pallas_call(functools.partial(time_kernel, base, size, extra), in_spec...  11.9 us
    pallas_call x1, Pallas kernels, scene_part(): pl.pallas_call(functools.partial(scene_kernel, parts, mlp, fetch), in_spe...  9.19 us
    all_to_all x1, waiting for transfers between devices, exchange(): lax.all_to_all(values, 'seq', split_axis=0, concat_axis=0, tiled=True)  2.04 us
  transfers between devices with their start and end apart: 1, of which 1 were waited for; matrix products, arithmetic and copies ran while one was open for 0% of the time, Pallas kernels for 9%

profile of v6, /device:TPU:1, one launch (start us, length us, event | category | flops | bytes accessed | tf_op | source)
XLA Modules:
  0.0 81.2 jit_solution(14920284296057143633)
XLA Ops:
  0.0 79.8 %conditional.1 = (bf16[32,32,512]{2,1,0:T(8,128)(2,1)S(1)}) conditional(s32[]{:T(128)} %convert_element_type.3, (s32[32]{0:T(128)}, bf16[16,64,512]{2,1,0:T(8,128)(2,1)}, f32[3,512]{1,0:T(4,128)}, bf16[512,1536]{1,0:T(8,128)(2,1)}, bf16[512,512]{1,0:T(8,128)(2,1)}, /*index=5*/bf16[512,1536]{1,0:T(8,128)(2,1)}, bf16[512,512]{1,0:T(8,128)(2,1)}, ...), branch_computations={%region_0.1_spmd, %region_1.2_spmd} | conditional | flops 21474836480 | bytes 39871096 | solution.py:409
  0.0 4.3 %time_part_0_4.1 = bf16[32,8,512]{2,1,0:T(8,128)(2,1)} custom-call(s32[32]{0:T(128)} %get-tuple-element.44.counts_hbm.counts, bf16[16,64,512]{2,1,0:T(8,128)(2,1)} %get-tuple-element.45.tokens_hbm, f32[3,512]{1,0:T(4,128)} %get-tuple-element.46.gains_hbm.refs_2_, bf16[512,1536]{1,0:T(8,128)(2,1)} %get-tuple-element.47.refs_0_, ...), custom_call_target="tpu_custom_call" | custom-call | flops 1610612736 | bytes 4194304 | tf_op jit(solution)/shard_map/cond/branch_0_fun/time_part_0_4/pallas_call | solution.py:176
  4.3 12.0 %all-to-all-start = ((bf16[32,8,512]{2,1,0:T(8,128)(2,1)}), bf16[32,8,512]{2,1,0:T(8,128)(2,1)S(1)}, u32[]{:S(2)}, u32[]{:S(2)}) async-start(bf16[32,8,512]{2,1,0:T(8,128)(2,1)} %time_part_0_4.1), calls=%async_computation | async-start | bytes 524288 | tf_op jit(solution)/shard_map/cond/branch_0_fun/all_to_all | solution.py:384
  16.3 7.6 %time_part_4_12.1 = (bf16[32,24,512]{2,1,0:T(8,128)(2,1)S(1)}, bf16[512,1536]{1,0:T(8,128)(2,1)S(1)}, bf16[512,512]{1,0:T(8,128)(2,1)S(1)}) custom-call(s32[32]{0:T(128)} %get-tuple-element.44.counts_hbm.counts, bf16[16,64,512]{2,1,0:T(8,128)(2,1)} %get-tuple-element.45.tokens_hbm, f32[3,512]{1,0:T(4,128)} %get-tuple-element.46.gains_hbm.refs_2_, ...), custom_call_target="tpu_custom_call" | custom-call | flops 4831838208 | bytes 4194304 | tf_op jit(solution)/shard_map/cond/branch_0_fun/time_part_4_12/pallas_call | solution.py:176
  23.9 0.0 copy-start.2
  23.9 0.0 copy-start.4
  24.0 2.0 %all-to-all-done.refs_0_ = bf16[32,8,512]{2,1,0:T(8,128)(2,1)S(1)} async-done(((bf16[32,8,512]{2,1,0:T(8,128)(2,1)}), bf16[32,8,512]{2,1,0:T(8,128)(2,1)S(1)}, u32[]{:S(2)}, u32[]{:S(2)}) %all-to-all-start) | async-done | bytes 262176 | tf_op jit(solution)/shard_map/cond/branch_0_fun/all_to_all | solution.py:384
  26.0 21.7 %all_to_all.20.refs_1_ = bf16[32,24,512]{2,1,0:T(8,128)(2,1)S(1)} all-to-all(bf16[32,24,512]{2,1,0:T(8,128)(2,1)S(1)} %get-tuple-element.51), channel_id=1, replica_groups=mesh['scene'=8,'seq'=32] {'seq'}, dimensions={0} | all-to-all | bytes 1572864 | tf_op jit(solution)/shard_map/cond/branch_0_fun/all_to_all | solution.py:384
  47.7 0.0 copy-done.2
  47.7 0.0 copy-done.4
  47.7 9.2 %scene_part_2.1 = bf16[32,32,512]{2,1,0:T(8,128)(2,1)S(1)} custom-call(s32[32]{0:T(128)S(1)} %copy-done.4, bf16[32,8,512]{2,1,0:T(8,128)(2,1)S(1)} %all-to-all-done.refs_0_, bf16[32,24,512]{2,1,0:T(8,128)(2,1)S(1)} %all_to_all.20.refs_1_, f32[3,512]{1,0:T(4,128)S(1)} %copy-done.2, bf16[512,1536]{1,0:T(8,128)(2,1)S(1)} %get-tuple-element.52.refs_3_, ...), custom_call_target="tpu_custom_call" | custom-call | flops 10737418240 | bytes 8388608 | tf_op jit(solution)/shard_map/cond/branch_0_fun/scene_part_2/pallas_call | solution.py:308
  56.9 22.9 %all_to_all.21 = bf16[32,32,512]{2,1,0:T(8,128)(2,1)S(1)} all-to-all(bf16[32,32,512]{2,1,0:T(8,128)(2,1)S(1)} %scene_part_2.1), channel_id=1, replica_groups=mesh['scene'=8,'seq'=32] {'seq'}, dimensions={0} | all-to-all | bytes 2097152 | tf_op jit(solution)/shard_map/cond/branch_0_fun/all_to_all | solution.py:384
  79.8 1.2 %order_part.1 = bf16[16,64,512]{2,1,0:T(8,128)(2,1)} custom-call(bf16[32,32,512]{2,1,0:T(8,128)(2,1)S(1)} %get-tuple-element.68.recv), custom_call_target="tpu_custom_call" | custom-call | tf_op jit(solution)/shard_map/order_part/pallas_call | solution.py:369
Async XLA Ops:
  4.3 21.7 %all-to-all-start = ((bf16[32,8,512]{2,1,0:T(8,128)(2,1)}), bf16[32,8,512]{2,1,0:T(8,128)(2,1)S(1)}, u32[]{:S(2)}, u32[]{:S(2)}) async-start(bf16[32,8,512]{2,1,0:T(8,128)(2,1)} %time_part_0_4.1), calls=%async_computation | async-start | bytes 524288 | tf_op jit(solution)/shard_map/cond/branch_0_fun/all_to_all | solution.py:384
  23.9 23.7 %copy-start.2 = (f32[3,512]{1,0:T(4,128)S(1)}, f32[3,512]{1,0:T(4,128)}, u32[]{:S(2)}) copy-start(f32[3,512]{1,0:T(4,128)} %get-tuple-element.46.gains_hbm.refs_2_) | copy-start | bytes 18436 | tf_op jit(solution)/shard_map/cond
  23.9 23.7 %copy-start.4 = (s32[32]{0:T(128)S(1)}, s32[32]{0:T(128)}, u32[]{:S(2)}) copy-start(s32[32]{0:T(128)} %get-tuple-element.44.counts_hbm.counts) | copy-start | bytes 388 | tf_op jit(solution)/shard_map/cond

commit v7 on v6

--- a/solution.py
+++ b/solution.py
@@ -386,7 +386,7 @@
 
 def one_exchange(counts, tokens, gains, qkv_time, out_time, *later):
     arrays, weights = (counts, tokens, gains), (qkv_time, out_time)
-    after_time, fetched = time_part(0, SLOTS, 8, arrays, weights, later=later[:2])
+    after_time, fetched = time_part(0, SLOTS, 16, arrays, weights, later=later[:2])
     recv = [exchange(after_time)]
     o2 = exchange(scene_part([(0, SLOTS)], recv, counts, gains, fetched, 0))
     return mlp_part(counts, after_time, o2, gains, *later[2:])

time: 82 us -> 82.1 us (level)
  Pallas kernels: 22.3 us -> 20.6 us
  waiting for transfers between devices: 2.04 us -> 3.72 us
    pallas_call x2, Pallas kernels: 11.9 us -> 10.2 us  [time_part(): pl.pallas_call(functools.partial(time_kernel, base, size, extra), in_spec...]
    all_to_all x1, waiting for transfers between devices: 2.04 us -> 3.72 us  [exchange(): lax.all_to_all(values, 'seq', split_axis=0, concat_axis=0, tiled=True)]
  transfers between devices with their start and end apart: 1 -> 1, of which waited for: 1 -> 1; matrix products, arithmetic and copies ran while one was open for 0% -> 0% of each run, Pallas kernels for 9% -> 7%
where the time goes in v7:
time: 82.1 us; the launch traced here: 81.8 us
  blocking collectives  45.2 us (55%)
  Pallas kernels  20.6 us (25%)
  starting transfers between devices  12 us (15%)
  waiting for transfers between devices  3.72 us (5%)
    all_to_all x2, blocking collectives, exchange(): lax.all_to_all(values, 'seq', split_axis=0, concat_axis=0, tiled=True)  45.2 us
    all_to_all x1, starting transfers between devices, exchange(): lax.all_to_all(values, 'seq', split_axis=0, concat_axis=0, tiled=True)  12 us
    pallas_call x2, Pallas kernels, time_part(): pl.pallas_call(functools.partial(time_kernel, base, size, extra), in_spec...  10.2 us
    pallas_call x1, Pallas kernels, scene_part(): pl.pallas_call(functools.partial(scene_kernel, parts, mlp, fetch), in_spe...  9.19 us
    all_to_all x1, waiting for transfers between devices, exchange(): lax.all_to_all(values, 'seq', split_axis=0, concat_axis=0, tiled=True)  3.72 us
  transfers between devices with their start and end apart: 1, of which 1 were waited for; matrix products, arithmetic and copies ran while one was open for 0% of the time, Pallas kernels for 7%

profile of v7, /device:TPU:1, one launch (start us, length us, event | category | flops | bytes accessed | tf_op | source)
XLA Modules:
  0.0 81.8 jit_solution(4109390378978969672)
XLA Ops:
  0.0 80.4 %conditional.1 = (bf16[32,32,512]{2,1,0:T(8,128)(2,1)S(1)}) conditional(s32[]{:T(128)} %convert_element_type.3, (s32[32]{0:T(128)}, bf16[16,64,512]{2,1,0:T(8,128)(2,1)}, f32[3,512]{1,0:T(4,128)}, bf16[512,1536]{1,0:T(8,128)(2,1)}, bf16[512,512]{1,0:T(8,128)(2,1)}, /*index=5*/bf16[512,1536]{1,0:T(8,128)(2,1)}, bf16[512,512]{1,0:T(8,128)(2,1)}, ...), branch_computations={%region_0.1_spmd, %region_1.2_spmd} | conditional | flops 21474836480 | bytes 39871096 | solution.py:409
  0.0 4.3 %time_part_0_4.1 = bf16[32,8,512]{2,1,0:T(8,128)(2,1)} custom-call(s32[32]{0:T(128)} %get-tuple-element.44.counts_hbm.counts, bf16[16,64,512]{2,1,0:T(8,128)(2,1)} %get-tuple-element.45.tokens_hbm, f32[3,512]{1,0:T(4,128)} %get-tuple-element.46.gains_hbm.refs_2_, bf16[512,1536]{1,0:T(8,128)(2,1)} %get-tuple-element.47.refs_0_, ...), custom_call_target="tpu_custom_call" | custom-call | flops 1610612736 | bytes 4194304 | tf_op jit(solution)/shard_map/cond/branch_0_fun/time_part_0_4/pallas_call | solution.py:176
  4.3 12.0 %all-to-all-start = ((bf16[32,8,512]{2,1,0:T(8,128)(2,1)}), bf16[32,8,512]{2,1,0:T(8,128)(2,1)S(1)}, u32[]{:S(2)}, u32[]{:S(2)}) async-start(bf16[32,8,512]{2,1,0:T(8,128)(2,1)} %time_part_0_4.1), calls=%async_computation | async-start | bytes 524288 | tf_op jit(solution)/shard_map/cond/branch_0_fun/all_to_all | solution.py:384
  16.3 5.9 %time_part_4_12.1 = (bf16[32,24,512]{2,1,0:T(8,128)(2,1)S(1)}, bf16[512,1536]{1,0:T(8,128)(2,1)S(1)}, bf16[512,512]{1,0:T(8,128)(2,1)S(1)}) custom-call(s32[32]{0:T(128)} %get-tuple-element.44.counts_hbm.counts, bf16[16,64,512]{2,1,0:T(8,128)(2,1)} %get-tuple-element.45.tokens_hbm, f32[3,512]{1,0:T(4,128)} %get-tuple-element.46.gains_hbm.refs_2_, ...), custom_call_target="tpu_custom_call" | custom-call | flops 4831838208 | bytes 4194304 | tf_op jit(solution)/shard_map/cond/branch_0_fun/time_part_4_12/pallas_call | solution.py:176
  22.2 0.0 copy-start.2
  22.3 0.0 copy-start.4
  22.3 3.7 %all-to-all-done.refs_0_ = bf16[32,8,512]{2,1,0:T(8,128)(2,1)S(1)} async-done(((bf16[32,8,512]{2,1,0:T(8,128)(2,1)}), bf16[32,8,512]{2,1,0:T(8,128)(2,1)S(1)}, u32[]{:S(2)}, u32[]{:S(2)}) %all-to-all-start) | async-done | bytes 262176 | tf_op jit(solution)/shard_map/cond/branch_0_fun/all_to_all | solution.py:384
  26.0 21.7 %all_to_all.20.refs_1_ = bf16[32,24,512]{2,1,0:T(8,128)(2,1)S(1)} all-to-all(bf16[32,24,512]{2,1,0:T(8,128)(2,1)S(1)} %get-tuple-element.51), channel_id=1, replica_groups=mesh['scene'=8,'seq'=32] {'seq'}, dimensions={0} | all-to-all | bytes 1572864 | tf_op jit(solution)/shard_map/cond/branch_0_fun/all_to_all | solution.py:384
  47.7 0.0 copy-done.2
  47.7 0.0 copy-done.4
  47.7 9.2 %scene_part_2.1 = bf16[32,32,512]{2,1,0:T(8,128)(2,1)S(1)} custom-call(s32[32]{0:T(128)S(1)} %copy-done.4, bf16[32,8,512]{2,1,0:T(8,128)(2,1)S(1)} %all-to-all-done.refs_0_, bf16[32,24,512]{2,1,0:T(8,128)(2,1)S(1)} %all_to_all.20.refs_1_, f32[3,512]{1,0:T(4,128)S(1)} %copy-done.2, bf16[512,1536]{1,0:T(8,128)(2,1)S(1)} %get-tuple-element.52.refs_3_, ...), custom_call_target="tpu_custom_call" | custom-call | flops 10737418240 | bytes 8388608 | tf_op jit(solution)/shard_map/cond/branch_0_fun/scene_part_2/pallas_call | solution.py:308
  56.9 23.5 %all_to_all.21 = bf16[32,32,512]{2,1,0:T(8,128)(2,1)S(1)} all-to-all(bf16[32,32,512]{2,1,0:T(8,128)(2,1)S(1)} %scene_part_2.1), channel_id=1, replica_groups=mesh['scene'=8,'seq'=32] {'seq'}, dimensions={0} | all-to-all | bytes 2097152 | tf_op jit(solution)/shard_map/cond/branch_0_fun/all_to_all | solution.py:384
  80.4 1.2 %order_part.1 = bf16[16,64,512]{2,1,0:T(8,128)(2,1)} custom-call(bf16[32,32,512]{2,1,0:T(8,128)(2,1)S(1)} %get-tuple-element.68.recv), custom_call_target="tpu_custom_call" | custom-call | tf_op jit(solution)/shard_map/order_part/pallas_call | solution.py:369
Async XLA Ops:
  4.3 21.7 %all-to-all-start = ((bf16[32,8,512]{2,1,0:T(8,128)(2,1)}), bf16[32,8,512]{2,1,0:T(8,128)(2,1)S(1)}, u32[]{:S(2)}, u32[]{:S(2)}) async-start(bf16[32,8,512]{2,1,0:T(8,128)(2,1)} %time_part_0_4.1), calls=%async_computation | async-start | bytes 524288 | tf_op jit(solution)/shard_map/cond/branch_0_fun/all_to_all | solution.py:384
  22.2 25.5 %copy-start.2 = (f32[3,512]{1,0:T(4,128)S(1)}, f32[3,512]{1,0:T(4,128)}, u32[]{:S(2)}) copy-start(f32[3,512]{1,0:T(4,128)} %get-tuple-element.46.gains_hbm.refs_2_) | copy-start | bytes 18436 | tf_op jit(solution)/shard_map/cond
  22.3 25.5 %copy-start.4 = (s32[32]{0:T(128)S(1)}, s32[32]{0:T(128)}, u32[]{:S(2)}) copy-start(s32[32]{0:T(128)} %get-tuple-element.44.counts_hbm.counts) | copy-start | bytes 388 | tf_op jit(solution)/shard_map/cond
